TPU v7x, 256 devices: a whole 4x4x8 slice. The times are simulated.
256 devices in a mesh: ta: 16 (over x_hi, y, core), gz: 16 (over z, x_lo).
Axes of the slice: x: 4 (x_hi: 2, x_lo: 2; x = x_hi * 2 + x_lo), y: 4, z: 8, core: 2. Of those that a mesh axis runs over, the one named last changes fastest.
Arguments:
- link_phases: float32 [3, 2, 48, 64, 128], P(None, None, 'ta', 'gz'), may hold values from -4 to 4
- active: int32 [48, 64, 128], P('ta', 'gz'), may hold values 0 or 1
- bin_index: int32 [2, 48, 64, 128], P(None, 'ta', 'gz'), may hold values from 0 to 7
- first_weight: bfloat16 [9, 32, 54], replicated, may hold values from -0.25 to 0.25
- first_bias: float32 [32], replicated, may hold values from -3 to 3
- second_weight: bfloat16 [9, 48, 288], replicated, may hold values from -0.125 to 0.125
- second_bias: float32 [48], replicated, may hold values from -3 to 3
- cotangent: float32 [2, 48, 64, 128], P(None, 'ta', 'gz'), may hold values from -6 to 6
- logdet_cotangent: float32 [48, 64, 128], P('ta', 'gz'), may hold values from -6 to 6
Outputs:
- link_grad: float32 [3, 2, 48, 64, 128], P(None, None, 'ta', 'gz')
- first_weight_grad: float32 [9, 32, 54], replicated
- first_bias_grad: float32 [32], replicated
- second_weight_grad: float32 [9, 48, 288], replicated
- second_bias_grad: float32 [48], replicated
All inputs are finite; a program needn't handle non-finite values. No bound on the sum of `active` on one device may be relied on, other than what follows from the above.
Results may differ from a plain program's by a relative error of at most 0.0064.
Values may be sent and summed in bfloat16 or wider, within the bound.
A program may use at most 128 MiB of HBM per device.

v0:
```python
import functools
import math

import jax
import jax.numpy as jnp
from jax import lax
from jax.experimental import pallas as pl
from jax.experimental.pallas import tpu as pltpu
from jax.sharding import PartitionSpec as P

K = 8
LT = 3
LZ = 4
LANES = 128
HID = 32
OUTC = 48
PLANES = LT * LZ
MESH_ID = pl.DeviceIdType.MESH

min_share = 0.001
min_deriv = 0.001
keep_share = 1.0 - K * min_share
two_pi = 2.0 * math.pi

f32 = jnp.float32
bf16 = jnp.bfloat16


def lane_x(rows):
    return lax.broadcasted_iota(jnp.int32, (rows, LANES), 1) % 8


def rolled(value, amount):
    amount = amount % LANES
    if amount == 0:
        return value
    return pltpu.roll(value, amount, 1)


def shifted(value, step_y, step_x):
    near = rolled(value, -(8 * step_y + step_x))
    if step_x == 0:
        return near
    xs = lane_x(value.shape[0])
    if step_x > 0:
        wrap = rolled(value, -(8 * step_y + step_x - 8))
        return jnp.where(xs < 8 - step_x, near, wrap)
    wrap = rolled(value, -(8 * step_y + step_x + 8))
    return jnp.where(xs >= -step_x, near, wrap)


def nine_shifts(value):
    return [shifted(value, sy, sx) for sy in (-1, 0, 1) for sx in (-1, 0, 1)]


def shift_sum(blocks):
    total = None
    for ix, dx in enumerate((-1, 0, 1)):
        part = None
        for iy, dy in enumerate((-1, 0, 1)):
            piece = rolled(blocks[3 * iy + ix], 8 * dy)
            part = piece if part is None else part + piece
        part = shifted(part, 0, -dx)
        total = part if total is None else total + part
    return total


def sin_cos(angle):
    turns = jnp.floor(angle * (2.0 / math.pi) + 0.5)
    rest = angle - turns * 1.5703125
    rest = rest - turns * 4.837512969970703125e-4
    rest = rest - turns * 7.54978995489188e-8
    sq = rest * rest
    s = rest + rest * sq * (-1.6666654611e-1 + sq * (8.3321608736e-3 - sq * 1.9515295891e-4))
    c = 1.0 - 0.5 * sq + sq * sq * (
        4.166664568298827e-2 + sq * (-1.388731625493765e-3 + sq * 2.443315711809948e-5)
    )
    quad = turns.astype(jnp.int32)
    swap = (quad & 1) == 1
    sin_v = jnp.where(swap, c, s)
    cos_v = jnp.where(swap, s, c)
    sin_v = jnp.where((quad & 2) == 2, -sin_v, sin_v)
    cos_v = jnp.where(((quad + 1) & 2) == 2, -cos_v, cos_v)
    return sin_v, cos_v


def loop_phases(x_two, y_two):
    plaq, wide, tall = [], [], []
    for x, y in zip(x_two, y_two):
        y_x = shifted(y, 0, 1)
        x_y = shifted(x, 1, 0)
        plaq.append(x + y_x - x_y - y)
        wide.append(x + shifted(x, 0, 1) + shifted(y, 0, 2) - shifted(x, 1, 1) - x_y - y)
        tall.append(x + y_x + shifted(y, 1, 1) - shifted(x, 2, 0) - shifted(y, 1, 0) - y)
    out = []
    for two in (plaq, wide, tall):
        out.append((two[0], two[1], -(two[0] + two[1])))
    return out


DIRS = [(dt, dz) for dt in (-1, 0, 1) for dz in (-1, 0, 1) if (dt, dz) != (0, 0)]


def neighbour(dt, dz):
    nt, nz = lax.axis_size("ta"), lax.axis_size("gz")
    mt, mz = lax.axis_index("ta"), lax.axis_index("gz")
    return (lax.rem(mt + dt + nt, nt), lax.rem(mz + dz + nz, nz))


def main_kernel(
    links, act, bins, w1p, b1, w2k, b2, wt2, wt1, cot, ldc,
    out_link, out_grad,
    lbuf, fs, fcols, pres, cols, sigs, red, coef, xab, pgs, pgr, pgv,
    pbuf, qbuf, fgs, g1s,
    send_l, recv_l, send_p, recv_p, send_q, recv_q, send_g, recv_g,
):
    barrier = pltpu.get_barrier_semaphore()
    for dt, dz in DIRS:
        pl.semaphore_signal(barrier, inc=1, device_id=neighbour(dt, dz), device_id_type=MESH_ID)

    for comp in range(4):
        for t in range(LT):
            lbuf[2 + t, pl.ds(8 + comp, LZ, stride=4), :] = links[pl.ds(comp * PLANES + t * LZ, LZ), :]
    pl.semaphore_wait(barrier, len(DIRS))

    t_from = {-1: slice(2, 4), 0: slice(2, 5), 1: slice(3, 5)}
    t_into = {-1: slice(5, 7), 0: slice(2, 5), 1: slice(0, 2)}
    z_from = {-1: slice(8, 16), 0: slice(8, 24), 1: slice(16, 24)}
    z_into = {-1: slice(24, 32), 0: slice(8, 24), 1: slice(0, 8)}
    link_copies = []
    for i, (dt, dz) in enumerate(DIRS):
        copy = pltpu.make_async_remote_copy(
            src_ref=lbuf.at[t_from[dt], z_from[dz]],
            dst_ref=lbuf.at[t_into[dt], z_into[dz]],
            send_sem=send_l.at[i], recv_sem=recv_l.at[i],
            device_id=neighbour(dt, dz), device_id_type=MESH_ID,
        )
        copy.start()
        link_copies.append(copy)
    fs[...] = jnp.zeros_like(fs)
    for copy in link_copies:
        copy.wait()

    def feature_slice(t, carry):
        x_two = [lbuf[t, pl.ds(comp, 8, stride=4), :] for comp in (0, 1)]
        y_two = [lbuf[t, pl.ds(comp, 8, stride=4), :] for comp in (2, 3)]
        for which, three in enumerate(loop_phases(x_two, y_two)):
            pairs = [sin_cos(psi) for psi in three]
            fs[pl.ds(2 * which, 8, stride=8), :] = (pairs[0][1] + pairs[1][1] + pairs[2][1]) * (1.0 / 3.0)
            fs[pl.ds(2 * which + 1, 8, stride=8), :] = (pairs[0][0] + pairs[1][0] + pairs[2][0]) * (1.0 / 3.0)
        row = pl.multiple_of(t * 80, 16)
        for z in range(8):
            blocks = nine_shifts(fs[z * 8 : z * 8 + 8, :])
            blocks.append(jnp.zeros((8, LANES), f32))
            fcols[pl.ds(row, 80), z * LANES : (z + 1) * LANES] = jnp.concatenate(blocks, axis=0).astype(bf16)
        return carry

    lax.fori_loop(0, 7, feature_slice, 0)

    def hidden_slice(t, carry):
        got = jnp.dot(
            w1p[...], fcols[pl.ds(pl.multiple_of(t * 80, 16), 240), :], preferred_element_type=f32
        )
        pre = got[0:32, 0:768] + got[32:64, 128:896] + got[64:96, 256:1024] + b1[...]
        pres[t] = pre[:, 128:640]
        hid = pre / (1.0 + jnp.exp(-pre))
        row = pl.multiple_of(t * 288, 16)
        for z in range(6):
            blocks = nine_shifts(hid[:, z * LANES : (z + 1) * LANES])
            cols[pl.ds(row, 288), z * LANES : (z + 1) * LANES] = jnp.concatenate(blocks, axis=0).astype(bf16)
        return carry

    lax.fori_loop(0, 5, hidden_slice, 0)

    level = lax.broadcasted_iota(jnp.int32, (K, LANES), 0)

    def param_slice(t, carry):
        got = jnp.dot(
            w2k[...], cols[pl.ds(pl.multiple_of(t * 288, 16), 864), :], preferred_element_type=f32
        )
        par = got[0:48, 0:512] + got[48:96, 128:640] + got[96:144, 256:768] + b2[...]
        grow = jnp.exp(-jnp.abs(par))
        soft = jnp.maximum(par, 0.0) + jnp.log1p(grow)
        sigs[t] = jnp.where(par >= 0.0, 1.0, grow) / (1.0 + grow)
        for z in range(LZ):
            for c in range(2):
                plane = t * LZ + z
                chosen = bins[pl.ds(c * PLANES + plane, 1), :]
                pick = level == chosen
                below = level < chosen
                after = level == ((chosen + 1) & 7)
                cut = soft[c * 24 : c * 24 + 24, z * LANES : (z + 1) * LANES]
                sw, sh, sd = cut[0:8], cut[8:16], cut[16:24]
                sums = (
                    sw, jnp.where(pick, sw, 0.0),
                    sh, jnp.where(pick, sh, 0.0), jnp.where(below, sh, 0.0),
                    jnp.where(pick, sd, 0.0), jnp.where(after, sd, 0.0),
                )
                for q, value in enumerate(sums):
                    red[q, pl.ds(c * 16 + plane, 1), :] = jnp.sum(value, axis=0, keepdims=True)
        return carry

    lax.fori_loop(0, LT, param_slice, 0)

    live = act[...].astype(f32)
    g_log = live * ldc[...]
    for c in range(2):
        x = links[c * 12 : c * 12 + 12, :]
        tl = links[48 + c * 12 : 60 + c * 12, :]
        xab[0:8, :] = links[c * 12 + 4 : c * 12 + 12, :]
        xab[8:12, :] = lbuf[5, pl.ds(8 + c, LZ, stride=4), :]
        theta = x + shifted(tl, 0, 1) - xab[0:12, :] - tl
        my_cot = cot[c * 12 : c * 12 + 12, :]
        g_new = -live * my_cot
        rows = slice(c * 16, c * 16 + 12)
        sum_w, pick_w = red[0, rows, :], red[1, rows, :]
        sum_h, pick_h, low_h = red[2, rows, :], red[3, rows, :], red[4, rows, :]
        d0 = min_deriv + red[5, rows, :]
        d1 = min_deriv + red[6, rows, :]
        inv_w, inv_h = 1.0 / sum_w, 1.0 / sum_h
        frac_w, frac_h, frac_low = pick_w * inv_w, pick_h * inv_h, low_h * inv_h
        width = min_share + keep_share * frac_w
        height = min_share + keep_share * frac_h
        r = height / width
        u = 1.0 / (1.0 + jnp.exp(-theta))
        v = 1.0 - u
        q = u * v
        den = r + (d0 + d1 - 2.0 * r) * q
        top = r * u * u + d0 * q
        numer = d1 * u * u + 2.0 * r * q + d0 * v * v
        inv_den = 1.0 / den
        g_top = g_new * two_pi * height * inv_den
        g_den = -(g_top * top + 2.0 * g_log) * inv_den
        g_num = g_log / numer
        g_h = g_new * two_pi * top * inv_den + g_log / height
        g_r = g_top * u * u + g_den * (1.0 - 2.0 * q) + 2.0 * g_num * q + g_log / r
        g_d0 = (g_top + g_den) * q + g_num * v * v
        g_d1 = g_den * q + g_num * u * u
        g_q = g_top * d0 + g_den * (d0 + d1 - 2.0 * r) + 2.0 * g_num * r
        g_u = 2.0 * g_top * r * u + 2.0 * g_num * (d1 * u - d0 * v) + g_q * (1.0 - 2.0 * u)
        g_theta = g_u * q + g_log * (1.0 - 2.0 * u)
        all_h = g_h + g_r / width
        all_w = -g_r * r / width
        base = two_pi * g_new
        a_w = keep_share * all_w * inv_w
        coef[0, rows, :] = a_w
        coef[1, rows, :] = a_w * frac_w
        coef[2, rows, :] = keep_share * all_h * inv_h
        coef[3, rows, :] = keep_share * base * inv_h
        coef[4, rows, :] = keep_share * (all_h * frac_h + base * frac_low) * inv_h
        coef[5, rows, :] = g_d0
        coef[6, rows, :] = g_d1
        grad = g_theta + live * my_cot
        pgv[c, 4:16, :] = grad
        pgs[c * 4 : c * 4 + 4, :] = grad[8:12, :]

    phase_copy = pltpu.make_async_remote_copy(
        src_ref=pgs, dst_ref=pgr, send_sem=send_g, recv_sem=recv_g,
        device_id=neighbour(1, 0), device_id_type=MESH_ID,
    )
    phase_copy.start()

    def param_grad_slice(t, total):
        for z in range(LZ):
            plane = t * LZ + z
            parts = []
            for c in range(2):
                chosen = bins[pl.ds(c * PLANES + plane, 1), :]
                pick = level == chosen
                below = level < chosen
                after = level == ((chosen + 1) & 7)
                a = [coef[k, pl.ds(c * 16 + plane, 1), :] for k in range(7)]
                sig = sigs[t, c * 24 : c * 24 + 24, z * LANES : (z + 1) * LANES]
                parts.append((jnp.where(pick, a[0], 0.0) - a[1]) * sig[0:8])
                parts.append((jnp.where(pick, a[2], jnp.where(below, a[3], 0.0)) - a[4]) * sig[8:16])
                parts.append((jnp.where(pick, a[5], jnp.where(after, a[6], 0.0))) * sig[16:24])
            grad = jnp.concatenate(parts, axis=0)
            pbuf[t + 1, z + 1] = grad.astype(bf16)
            total = total + grad
        return total

    bias2 = jnp.sum(
        lax.fori_loop(0, LT, param_grad_slice, jnp.zeros((OUTC, LANES), f32)), axis=1, keepdims=True
    )

    h_from = {-1: slice(1, 2), 0: slice(1, 4), 1: slice(3, 4)}
    h_into = {-1: slice(4, 5), 0: slice(1, 4), 1: slice(0, 1)}
    v_from = {-1: slice(1, 2), 0: slice(1, 5), 1: slice(4, 5)}
    v_into = {-1: slice(5, 6), 0: slice(1, 5), 1: slice(0, 1)}

    def send_halo(buf, send, recv):
        copies = []
        for i, (dt, dz) in enumerate(DIRS):
            copy = pltpu.make_async_remote_copy(
                src_ref=buf.at[h_from[dt], v_from[dz]],
                dst_ref=buf.at[h_into[dt], v_into[dz]],
                send_sem=send.at[i], recv_sem=recv.at[i],
                device_id=neighbour(dt, dz), device_id_type=MESH_ID,
            )
            copy.start()
            copies.append(copy)
        return copies

    param_copies = send_halo(pbuf, send_p, recv_p)

    def spread(buf, t, rows):
        own = jnp.concatenate([buf[t + 1, z + 1] for z in range(LZ)], axis=1)
        one = jnp.zeros((rows, LANES), bf16)
        two = jnp.zeros((rows, 2 * LANES), bf16)
        return jnp.concatenate(
            [
                jnp.concatenate([own, two], axis=1),
                jnp.concatenate([one, own, one], axis=1),
                jnp.concatenate([two, own], axis=1),
            ],
            axis=0,
        )

    nt_dims = (((1,), (1,)), ((), ()))
    spread_p = [spread(pbuf, t, OUTC) for t in range(LT)]
    g2 = []
    for i in range(3):
        total = None
        for t in range(LT):
            part = lax.dot_general(
                spread_p[t], cols[(t + i) * 288 : (t + i + 1) * 288, :], nt_dims, preferred_element_type=f32
            )
            total = part if total is None else total + part
        g2.append(total)
        out_grad[i * 144 : (i + 1) * 144, 0:256] = total[:, 0:256].astype(bf16)
        g1s[i * 144 : (i + 1) * 144, 0:32] = total[:, 256:288]

    for copy in param_copies:
        copy.wait()

    def stacked(buf, t):
        rows = []
        for i in range(3):
            for j in range(3):
                rows.append(jnp.concatenate([buf[t + 2 - i, z + 2 - j] for z in range(LZ)], axis=1))
        return jnp.concatenate(rows, axis=0)

    def hidden_grad_slice(t, total):
        got = jnp.dot(wt2[...], stacked(pbuf, t), preferred_element_type=f32)
        for z in range(LZ):
            lanes = slice(z * LANES, (z + 1) * LANES)
            grad = shift_sum([got[b * HID : (b + 1) * HID, lanes] for b in range(9)])
            pre = pres[t + 1, :, lanes]
            sig = 1.0 / (1.0 + jnp.exp(-pre))
            grad = grad * (sig * (1.0 + pre * (1.0 - sig)))
            qbuf[t + 1, z + 1] = grad.astype(bf16)
            total = total + grad
        return total

    bias1 = jnp.sum(
        lax.fori_loop(0, LT, hidden_grad_slice, jnp.zeros((HID, LANES), f32)), axis=1, keepdims=True
    )

    preact_copies = send_halo(qbuf, send_q, recv_q)

    spread_q = [spread(qbuf, t, HID) for t in range(LT)]
    g1 = []
    for i in range(3):
        total = None
        for t in range(LT):
            row = (t + 1 + i) * 80
            part = lax.dot_general(
                spread_q[t], fcols[row : row + 80, 128:896], nt_dims, preferred_element_type=f32
            )
            total = part if total is None else total + part
        g1.append(jnp.concatenate([total, jnp.zeros((96, 48), f32)], axis=1))
    first = jnp.concatenate(
        [pltpu.roll(g, 48, 1) for g in g1] + [jnp.zeros((144, LANES), f32)], axis=0
    )
    bias = jnp.concatenate([bias2, bias1, jnp.zeros((432 - 80, 1), f32)], axis=0)
    lane = lax.broadcasted_iota(jnp.int32, (432, LANES), 1)
    tail = jnp.where(lane < 32, g1s[...], jnp.where(lane == 32, bias, first))
    out_grad[0:432, 256:384] = tail.astype(bf16)
    out_grad[432:512, :] = jnp.zeros((80, 384), bf16)

    x_two = [links[0:12, :], links[12:24, :]]
    y_two = [links[24:36, :], links[36:48, :]]
    pairs = [[sin_cos(psi) for psi in three] for three in loop_phases(x_two, y_two)]

    phase_copy.wait()
    for copy in preact_copies:
        copy.wait()

    def feature_grad_slice(t, carry):
        got = jnp.dot(wt1[...], stacked(qbuf, t), preferred_element_type=f32)
        for z in range(LZ):
            lanes = slice(z * LANES, (z + 1) * LANES)
            grad = shift_sum([got[b * 8 : (b + 1) * 8, lanes] for b in range(9)])
            fgs[pl.ds(pl.multiple_of((t * LZ + z) * 8, 8), 8), :] = grad
        return carry

    lax.fori_loop(0, LT, feature_grad_slice, 0)

    third = 1.0 / 3.0
    loop_grads = []
    for which in range(3):
        g_cos = fgs[pl.ds(2 * which, PLANES, stride=8), :] * third
        g_sin = fgs[pl.ds(2 * which + 1, PLANES, stride=8), :] * third
        three = [g_sin * cos_v - g_cos * sin_v for sin_v, cos_v in pairs[which]]
        loop_grads.append((three[0] - three[2], three[1] - three[2]))
    for c in range(2):
        dp, dw, dr = loop_grads[0][c], loop_grads[1][c], loop_grads[2][c]
        side = dp + dr
        x_ctx = (
            dp + dw + dr
            - shifted(dp + dw, -1, 0)
            + shifted(dw, 0, -1)
            - shifted(dw, -1, -1)
            - shifted(dr, -2, 0)
        )
        y_ctx = (
            shifted(side, 0, -1)
            - side
            - dw
            + shifted(dw, 0, -2)
            + shifted(dr, -1, -1)
            - shifted(dr, -1, 0)
        )
        pgv[c, 0:4, :] = pgr[c * 4 : c * 4 + 4, :]
        grad = pgv[c, 4:16, :]
        prev = pgv[c, 0:12, :]
        out_link[c * 12 : c * 12 + 12, :] = grad - prev + x_ctx
        out_link[24 + c * 12 : 36 + c * 12, :] = y_ctx
        out_link[48 + c * 12 : 60 + c * 12, :] = cot[c * 12 : c * 12 + 12, :] - grad + shifted(grad, 0, -1)


def sum_kernel(scale, grad, out, got1, mid, got2, fin, send1, recv1, send2, recv2, send3, recv3):
    nt, nz = lax.axis_size("ta"), lax.axis_size("gz")
    mt, mz = lax.axis_index("ta"), lax.axis_index("gz")
    rows = grad.shape[0] // nt
    barrier = pltpu.get_barrier_semaphore()
    for k in range(1, nt):
        pl.semaphore_signal(barrier, inc=1, device_id=(lax.rem(mt + k, nt), mz), device_id_type=MESH_ID)
    for k in range(1, nz):
        pl.semaphore_signal(barrier, inc=1, device_id=(mt, lax.rem(mz + k, nz)), device_id_type=MESH_ID)
    pl.semaphore_wait(barrier, nt + nz - 2)

    copies = []
    for k in range(1, nt):
        peer = lax.rem(mt + k, nt)
        copy = pltpu.make_async_remote_copy(
            src_ref=grad.at[pl.ds(pl.multiple_of(peer * rows, 16), rows)],
            dst_ref=got1.at[k],
            send_sem=send1.at[k], recv_sem=recv1.at[k],
            device_id=(peer, mz), device_id_type=MESH_ID,
        )
        copy.start()
        copies.append(copy)
    total = grad[pl.ds(pl.multiple_of(mt * rows, 16), rows), :].astype(f32)
    for k, copy in enumerate(copies):
        copy.wait()
        total = total + got1[k + 1].astype(f32)
    mid[...] = (total * scale).astype(bf16)

    copies = []
    for k in range(1, nz):
        peer = lax.rem(mz + k, nz)
        copy = pltpu.make_async_remote_copy(
            src_ref=mid, dst_ref=got2.at[mz],
            send_sem=send2.at[k], recv_sem=recv2.at[k],
            device_id=(mt, peer), device_id_type=MESH_ID,
        )
        copy.start()
        copies.append(copy)
    got2[mz] = mid[...]
    for copy in copies:
        copy.wait()
    total = got2[0].astype(f32)
    for k in range(1, nz):
        total = total + got2[k].astype(f32)
    fin[...] = total.astype(bf16)

    copies = []
    mine = pl.ds(pl.multiple_of(mt * rows, 16), rows)
    for k in range(1, nt):
        peer = lax.rem(mt + k, nt)
        copy = pltpu.make_async_remote_copy(
            src_ref=fin, dst_ref=out.at[mine],
            send_sem=send3.at[k], recv_sem=recv3.at[k],
            device_id=(peer, mz), device_id_type=MESH_ID,
        )
        copy.start()
        copies.append(copy)
    out[mine, :] = fin[...]
    for copy in copies:
        copy.wait()


def vmem():
    return pl.BlockSpec(memory_space=pltpu.VMEM)


def local(
    link_phases, active, bin_index, first_weight, first_bias,
    second_weight, second_bias, cotangent, logdet_cotangent,
):
    nt, nz = lax.axis_size("ta"), lax.axis_size("gz")
    fw = first_weight.reshape(3, 3, HID, 9, 6)
    fw = jnp.pad(fw, ((0, 0), (0, 0), (0, 0), (0, 0), (0, 2))).reshape(3, 96, 72)
    wt1 = fw.reshape(288, 72).T
    w1p = jnp.pad(fw, ((0, 0), (0, 0), (0, 8))).transpose(1, 0, 2).reshape(96, 240)
    w2k = second_weight.reshape(3, 144, 288).transpose(1, 0, 2).reshape(144, 864)
    wt2 = second_weight.reshape(432, 288).T

    dma = pltpu.SemaphoreType.DMA
    out_link, out_grad = pl.pallas_call(
        main_kernel,
        out_shape=(
            jax.ShapeDtypeStruct((72, LANES), f32),
            jax.ShapeDtypeStruct((512, 384), bf16),
        ),
        in_specs=[vmem()] * 11,
        out_specs=(vmem(), vmem()),
        scratch_shapes=[
            pltpu.VMEM((7, 32, LANES), f32),
            pltpu.VMEM((64, LANES), f32),
            pltpu.VMEM((560, 1024), bf16),
            pltpu.VMEM((5, HID, 512), f32),
            pltpu.VMEM((1440, 768), bf16),
            pltpu.VMEM((LT, OUTC, 512), f32),
            pltpu.VMEM((7, 32, LANES), f32),
            pltpu.VMEM((7, 32, LANES), f32),
            pltpu.VMEM((16, LANES), f32),
            pltpu.VMEM((8, LANES), f32),
            pltpu.VMEM((8, LANES), f32),
            pltpu.VMEM((2, 16, LANES), f32),
            pltpu.VMEM((5, 6, OUTC, LANES), bf16),
            pltpu.VMEM((5, 6, HID, LANES), bf16),
            pltpu.VMEM((96, LANES), f32),
            pltpu.VMEM((432, LANES), f32),
            dma((8,)), dma((8,)), dma((8,)), dma((8,)), dma((8,)), dma((8,)), dma, dma,
        ],
        compiler_params=pltpu.CompilerParams(
            collective_id=0, has_side_effects=True, vmem_limit_bytes=40 * 1024 * 1024
        ),
        name="main_kernel",
    )(
        link_phases.reshape(72, LANES),
        active.reshape(PLANES, LANES),
        bin_index.reshape(2 * PLANES, LANES),
        w1p, first_bias.reshape(HID, 1), w2k, second_bias.reshape(OUTC, 1), wt2, wt1,
        cotangent.reshape(2 * PLANES, LANES),
        logdet_cotangent.reshape(PLANES, LANES),
    )

    rows = 512 // nt
    scale = 1.0 / math.sqrt(nt * nz * PLANES * LANES)
    summed = pl.pallas_call(
        functools.partial(sum_kernel, scale),
        out_shape=jax.ShapeDtypeStruct((512, 384), bf16),
        in_specs=[vmem()],
        out_specs=vmem(),
        scratch_shapes=[
            pltpu.VMEM((nt, rows, 384), bf16),
            pltpu.VMEM((rows, 384), bf16),
            pltpu.VMEM((nz, rows, 384), bf16),
            pltpu.VMEM((rows, 384), bf16),
            dma((nt,)), dma((nt,)), dma((nz,)), dma((nz,)), dma((nt,)), dma((nt,)),
        ],
        compiler_params=pltpu.CompilerParams(
            collective_id=1, has_side_effects=True, vmem_limit_bytes=40 * 1024 * 1024
        ),
        name="sum_kernel",
    )(out_grad)
    second = summed[0:432, 0:288].astype(f32).reshape(9, OUTC, 288)
    first = summed[0:288, 304:376].astype(f32).reshape(9, HID, 9, 8)[..., 0:6].reshape(9, HID, 54)
    bias = summed[0:80, 288].astype(f32)
    return (out_link.reshape(3, 2, LT, LZ, LANES), first, bias[48:80], second, bias[0:48])


def solution(mesh):
    return jax.shard_map(
        local,
        mesh=mesh,
        in_specs=(
            P(None, None, "ta", "gz", None),
            P("ta", "gz", None),
            P(None, "ta", "gz", None),
            P(), P(), P(), P(),
            P(None, "ta", "gz", None),
            P("ta", "gz", None),
        ),
        out_specs=(P(None, None, "ta", "gz", None), P(), P(), P(), P()),
        check_vma=False,
    )
```

profile of v0, /device:TPU:1, one launch (start us, length us, event | category | flops | bytes accessed | tf_op | source)
XLA Modules:
  0.0 73.6 jit_solution(4783357483803988517)
XLA Ops:
  0.6 0.0 copy-start.4
  0.6 0.7 reshape.72.act
  1.4 0.7 reshape.83.ldc
  2.1 0.7 copy.37.b1
  2.8 0.7 %copy.38.b2 = f32[48,1]{1,0:T(8,128)S(1)} copy(f32[48,1]{0,1:T(1,128)} %bitcast.40) | data formatting | bytes 384 | tf_op jit(solution)/shard_map/reshape | solution.py:546
  3.5 0.0 copy-done.4
  3.6 0.2 copy.31
  3.7 0.1 reshape.74
  3.8 0.1 copy.35
  3.9 0.2 reshape_reshape.3
  4.1 0.1 copy.32
  4.2 0.0 copy-start.3
  4.2 0.1 reshape.75
  4.4 0.1 copy.36.w1p
  4.5 0.7 copy-done.3
  5.2 0.2 copy.34
  5.3 0.2 copy.45
  5.5 0.0 copy-start
  5.5 0.0 copy-start.1
  5.5 0.0 copy-start.2
  5.5 0.3 reshape.79.w2k
  5.8 0.5 copy-done
  6.3 0.0 copy-done.1
  6.3 0.0 copy-done.2
  6.3 33.6 %main_kernel.1 = (f32[72,128]{1,0:T(8,128)S(1)}, bf16[512,384]{1,0:T(8,128)(2,1)S(1)}) custom-call(f32[72,128]{1,0:T(8,128)S(1)} %bitcast.30, s32[12,128]{1,0:T(8,128)S(1)} %reshape.72.act, s32[24,128]{1,0:T(8,128)S(1)} %bitcast.32, bf16[96,240]{1,0:T(8,128)(2,1)S(1)} %copy.36.w1p, f32[32,1]{1,0:T(8,128)S(1)} %copy.37.b1, bf16[144,864]{1,0:T(8,128)(2,1)S(1)} %reshape.79.w2k, ...), custom_call_target="tpu_custom_call" | custom-call | tf_op jit(solution)/shard_map/main_kernel/pallas_call | solution.py:511
  39.9 29.5 %sum_kernel.1 = bf16[512,384]{1,0:T(8,128)(2,1)S(1)} custom-call(bf16[512,384]{1,0:T(8,128)(2,1)S(1)} %get-tuple-element.8.grad), custom_call_target="tpu_custom_call" | custom-call | tf_op jit(solution)/shard_map/sum_kernel/pallas_call | solution.py:553
  69.4 0.1 slice_convert_fusion
  69.5 0.6 slice_reduce_fusion
  70.1 0.6 slice_reduce_fusion.1
  70.7 0.1 slice.25
  70.9 0.1 copy.39
  71.0 0.2 reshape.85
  71.3 0.8 %copy.41 = f32[9,32,54]{2,1,0:T(8,128)} copy(f32[9,32,54]{1,2,0:T(8,128)S(1)} %reshape.91) | data formatting | bytes 124416
  72.1 0.9 %convert.4 = f32[9,48,288]{2,1,0:T(8,128)} convert(bf16[9,48,288]{2,1,0:T(8,128)(2,1)S(1)} %bitcast.37) | non-fusion elementwise | flops 124416 | bytes 746496 | tf_op jit(solution)/shard_map/reshape | solution.py:570
  73.0 0.6 copy.47
  (6 shorter events, 0.2 us)
Async XLA Ops:
  0.6 2.9 %copy-start.4 = (bf16[9,32,54]{2,1,0:T(8,128)(2,1)S(1)}, bf16[9,32,54]{2,1,0:T(8,128)(2,1)}, u32[]{:S(2)}) copy-start(bf16[9,32,54]{2,1,0:T(8,128)(2,1)} %param.12) | copy-start | bytes 93316
  4.2 1.0 %copy-start.3 = (bf16[9,48,288]{2,1,0:T(8,128)(2,1)S(1)}, bf16[9,48,288]{2,1,0:T(8,128)(2,1)}, u32[]{:S(2)}) copy-start(bf16[9,48,288]{2,1,0:T(8,128)(2,1)} %param.14) | copy-start | bytes 746500
  5.5 0.8 %copy-start = (f32[3,2,3,4,128]{4,3,2,1,0:T(4,128)S(1)}, f32[3,2,3,4,128]{4,3,2,1,0:T(4,128)}, u32[]{:S(2)}) copy-start(f32[3,2,3,4,128]{4,3,2,1,0:T(4,128)} %param.9) | copy-start | bytes 110596
  5.5 0.8 %copy-start.1 = (s32[2,3,4,128]{3,2,1,0:T(4,128)S(1)}, s32[2,3,4,128]{3,2,1,0:T(4,128)}, u32[]{:S(2)}) copy-start(s32[2,3,4,128]{3,2,1,0:T(4,128)} %param.11) | copy-start | bytes 36868
  5.5 0.8 %copy-start.2 = (f32[2,3,4,128]{3,2,1,0:T(4,128)S(1)}, f32[2,3,4,128]{3,2,1,0:T(4,128)}, u32[]{:S(2)}) copy-start(f32[2,3,4,128]{3,2,1,0:T(4,128)} %param.16) | copy-start | bytes 36868
where the time goes:
time: 73.9 us; the launch traced here: 73.6 us
  Pallas kernels  63.1 us (85%)
  local copies, waits for them, and re-layouts  8.67 us (12%)
  other arithmetic  1 us (1%)
  between operations  0.82 us (1%)
    pallas_call x1, Pallas kernels, local(): pl.pallas_call(main_kernel, out_shape=(jax.ShapeDtypeStruct((72, LANES),...  33.6 us
    pallas_call x1, Pallas kernels, local(): pl.pallas_call(functools.partial(sum_kernel, scale), out_shape=jax.ShapeD...  29.5 us
    unnamed x13, local copies, waits for them, and re-layouts  2.77 us

commit v1 on v0

--- a/solution.py
+++ b/solution.py
@@ -108,20 +108,49 @@
 
 
 def main_kernel(
-    links, act, bins, w1p, b1, w2k, b2, wt2, wt1, cot, ldc,
-    out_link, out_grad,
+    scale, links, act, bins_in, first_w, b1, second_w, b2, cot_in, ldc_in,
+    out_link, out2, out1,
+    lk, bins, cot, site, w1p, w2k, wt2, wt1,
     lbuf, fs, fcols, pres, cols, sigs, red, coef, xab, pgs, pgr, pgv,
-    pbuf, qbuf, fgs, g1s,
+    pbuf, qbuf, fgs, tails, gm2, got_a, mid_b, got_b, part_c, all_c, fin_d,
+    gm1, got_e, mid_f, got_f, fin_g,
     send_l, recv_l, send_p, recv_p, send_q, recv_q, send_g, recv_g,
+    send_a, recv_a, send_b, recv_b, send_c, recv_c, send_d, recv_d,
+    send_e, recv_e, send_f, recv_f, send_h, recv_h,
 ):
+    nt, nz = lax.axis_size("ta"), lax.axis_size("gz")
+    mt, mz = lax.axis_index("ta"), lax.axis_index("gz")
     barrier = pltpu.get_barrier_semaphore()
-    for dt, dz in DIRS:
+    corners = [(dt, dz) for dt, dz in DIRS if dt != 0 and dz != 0]
+    for dt, dz in corners:
         pl.semaphore_signal(barrier, inc=1, device_id=neighbour(dt, dz), device_id_type=MESH_ID)
-
+    for k in range(1, nt):
+        pl.semaphore_signal(barrier, inc=1, device_id=(lax.rem(mt + k, nt), mz), device_id_type=MESH_ID)
+    for k in range(1, nz):
+        pl.semaphore_signal(barrier, inc=1, device_id=(mt, lax.rem(mz + k, nz)), device_id_type=MESH_ID)
+
+    def to_others(axis, src, dst, send, recv):
+        count, me = (nt, mt) if axis == "ta" else (nz, mz)
+        copies = []
+        for k in range(1, count):
+            peer = lax.rem(me + k, count)
+            copy = pltpu.make_async_remote_copy(
+                src_ref=src(peer), dst_ref=dst(k),
+                send_sem=send.at[k], recv_sem=recv.at[k],
+                device_id=(peer, mz) if axis == "ta" else (mt, peer), device_id_type=MESH_ID,
+            )
+            copy.start()
+            copies.append(copy)
+        return copies
+
+    for d in range(3):
+        for c in range(2):
+            for t in range(LT):
+                lk[pl.ds(d * 24 + c * 12 + t * 4, LZ), :] = links[d, c, t]
     for comp in range(4):
         for t in range(LT):
-            lbuf[2 + t, pl.ds(8 + comp, LZ, stride=4), :] = links[pl.ds(comp * PLANES + t * LZ, LZ), :]
-    pl.semaphore_wait(barrier, len(DIRS))
+            lbuf[2 + t, pl.ds(8 + comp, LZ, stride=4), :] = lk[pl.ds(comp * PLANES + t * LZ, LZ), :]
+    pl.semaphore_wait(barrier, nt + nz - 2 + len(corners))
 
     t_from = {-1: slice(2, 4), 0: slice(2, 5), 1: slice(3, 5)}
     t_into = {-1: slice(5, 7), 0: slice(2, 5), 1: slice(0, 2)}
@@ -138,6 +167,48 @@
         copy.start()
         link_copies.append(copy)
     fs[...] = jnp.zeros_like(fs)
+
+    for t in range(LT):
+        site[0, pl.ds(t * LZ, LZ), :] = act[t].astype(f32)
+        site[1, pl.ds(t * LZ, LZ), :] = ldc_in[t]
+        for c in range(2):
+            bins[pl.ds(c * 12 + t * LZ, LZ), :] = bins_in[c, t]
+            cot[pl.ds(c * 12 + t * LZ, LZ), :] = cot_in[c, t]
+    nt_dims = (((1,), (1,)), ((), ()))
+
+    def one_hot(rows, padded_dim):
+        shape = (rows, 54) if padded_dim == 0 else (54, rows)
+        wide = lax.broadcasted_iota(jnp.int32, shape, padded_dim)
+        tight = lax.broadcasted_iota(jnp.int32, shape, 1 - padded_dim)
+        hit = (wide < 72) & (wide % 8 < 6) & (tight == (wide // 8) * 6 + wide % 8)
+        return jnp.where(hit, 1.0, 0.0).astype(bf16)
+
+    spread80 = one_hot(80, 1)
+    w1p[...] = jnp.concatenate(
+        [
+            jnp.dot(first_w[i * 96 : (i + 1) * 96, :], spread80, preferred_element_type=f32)
+            for i in range(3)
+        ],
+        axis=1,
+    ).astype(bf16)
+    wt1[...] = lax.dot_general(
+        one_hot(72, 0), first_w[...], nt_dims, preferred_element_type=f32
+    ).astype(bf16)
+    w2k[...] = jnp.concatenate(
+        [second_w[i * 144 : (i + 1) * 144, :].astype(f32) for i in range(3)], axis=1
+    ).astype(bf16)
+    diag = lax.broadcasted_iota(jnp.int32, (288, 288), 0) == lax.broadcasted_iota(jnp.int32, (288, 288), 1)
+    wt2[...] = lax.dot_general(
+        jnp.where(diag, 1.0, 0.0).astype(bf16), second_w[...], nt_dims, preferred_element_type=f32
+    ).astype(bf16)
+
+    def as_column(row_ref, count):
+        eye = lax.broadcasted_iota(jnp.int32, (count, count), 0) == lax.broadcasted_iota(
+            jnp.int32, (count, count), 1
+        )
+        return jnp.sum(jnp.where(eye, row_ref[...], 0.0), axis=1, keepdims=True)
+
+    b1_col, b2_col = as_column(b1, HID), as_column(b2, OUTC)
     for copy in link_copies:
         copy.wait()
 
@@ -161,7 +232,7 @@
         got = jnp.dot(
             w1p[...], fcols[pl.ds(pl.multiple_of(t * 80, 16), 240), :], preferred_element_type=f32
         )
-        pre = got[0:32, 0:768] + got[32:64, 128:896] + got[64:96, 256:1024] + b1[...]
+        pre = got[0:32, 0:768] + got[32:64, 128:896] + got[64:96, 256:1024] + b1_col
         pres[t] = pre[:, 128:640]
         hid = pre / (1.0 + jnp.exp(-pre))
         row = pl.multiple_of(t * 288, 16)
@@ -178,7 +249,7 @@
         got = jnp.dot(
             w2k[...], cols[pl.ds(pl.multiple_of(t * 288, 16), 864), :], preferred_element_type=f32
         )
-        par = got[0:48, 0:512] + got[48:96, 128:640] + got[96:144, 256:768] + b2[...]
+        par = got[0:48, 0:512] + got[48:96, 128:640] + got[96:144, 256:768] + b2_col
         grow = jnp.exp(-jnp.abs(par))
         soft = jnp.maximum(par, 0.0) + jnp.log1p(grow)
         sigs[t] = jnp.where(par >= 0.0, 1.0, grow) / (1.0 + grow)
@@ -202,12 +273,12 @@
 
     lax.fori_loop(0, LT, param_slice, 0)
 
-    live = act[...].astype(f32)
-    g_log = live * ldc[...]
+    live = site[0, 0:12, :]
+    g_log = live * site[1, 0:12, :]
     for c in range(2):
-        x = links[c * 12 : c * 12 + 12, :]
-        tl = links[48 + c * 12 : 60 + c * 12, :]
-        xab[0:8, :] = links[c * 12 + 4 : c * 12 + 12, :]
+        x = lk[c * 12 : c * 12 + 12, :]
+        tl = lk[48 + c * 12 : 60 + c * 12, :]
+        xab[0:8, :] = lk[c * 12 + 4 : c * 12 + 12, :]
         xab[8:12, :] = lbuf[5, pl.ds(8 + c, LZ, stride=4), :]
         theta = x + shifted(tl, 0, 1) - xab[0:12, :] - tl
         my_cot = cot[c * 12 : c * 12 + 12, :]
@@ -316,9 +387,7 @@
             axis=0,
         )
 
-    nt_dims = (((1,), (1,)), ((), ()))
     spread_p = [spread(pbuf, t, OUTC) for t in range(LT)]
-    g2 = []
     for i in range(3):
         total = None
         for t in range(LT):
@@ -326,9 +395,24 @@
                 spread_p[t], cols[(t + i) * 288 : (t + i + 1) * 288, :], nt_dims, preferred_element_type=f32
             )
             total = part if total is None else total + part
-        g2.append(total)
-        out_grad[i * 144 : (i + 1) * 144, 0:256] = total[:, 0:256].astype(bf16)
-        g1s[i * 144 : (i + 1) * 144, 0:32] = total[:, 256:288]
+        gm2[i * 144 : (i + 1) * 144, :] = total[:, 0:128].astype(bf16)
+        gm2[432 + i * 144 : 576 + i * 144, :] = total[:, 128:256].astype(bf16)
+        tails[i * 144 : (i + 1) * 144, :] = jnp.concatenate(
+            [total[:, 256:288], jnp.zeros((144, 96), f32)], axis=1
+        )
+    tails[432:448, :] = jnp.zeros((16, LANES), f32)
+    tail = tails[0:112, :]
+    for g in range(1, 4):
+        tail = tail + pltpu.roll(tails[g * 112 : (g + 1) * 112, :], 32 * g, 1)
+    gm2[864:976, :] = tail.astype(bf16)
+    gm2[976:1024, :] = jnp.zeros((48, LANES), bf16)
+
+    rows2 = 1024 // nt
+    rows_part = rows2 // nz
+    copies_a = to_others(
+        "ta", lambda peer: gm2.at[pl.ds(pl.multiple_of(peer * rows2, 16), rows2)],
+        lambda k: got_a.at[k], send_a, recv_a,
+    )
 
     for copy in param_copies:
         copy.wait()
@@ -358,6 +442,16 @@
 
     preact_copies = send_halo(qbuf, send_q, recv_q)
 
+    total = gm2[pl.ds(pl.multiple_of(mt * rows2, 16), rows2), :].astype(f32)
+    for k, copy in enumerate(copies_a):
+        copy.wait()
+        total = total + got_a[k + 1].astype(f32)
+    total = total * scale
+    for p in range(nz):
+        mid_b[p] = total[p * rows_part : (p + 1) * rows_part, :]
+    copies_b = to_others("gz", lambda peer: mid_b.at[peer], lambda k: got_b.at[k], send_b, recv_b)
+
+    tight80 = one_hot(80, 0)
     spread_q = [spread(qbuf, t, HID) for t in range(LT)]
     g1 = []
     for i in range(3):
@@ -368,19 +462,30 @@
                 spread_q[t], fcols[row : row + 80, 128:896], nt_dims, preferred_element_type=f32
             )
             total = part if total is None else total + part
-        g1.append(jnp.concatenate([total, jnp.zeros((96, 48), f32)], axis=1))
-    first = jnp.concatenate(
-        [pltpu.roll(g, 48, 1) for g in g1] + [jnp.zeros((144, LANES), f32)], axis=0
-    )
-    bias = jnp.concatenate([bias2, bias1, jnp.zeros((432 - 80, 1), f32)], axis=0)
-    lane = lax.broadcasted_iota(jnp.int32, (432, LANES), 1)
-    tail = jnp.where(lane < 32, g1s[...], jnp.where(lane == 32, bias, first))
-    out_grad[0:432, 256:384] = tail.astype(bf16)
-    out_grad[432:512, :] = jnp.zeros((80, 384), bf16)
-
-    x_two = [links[0:12, :], links[12:24, :]]
-    y_two = [links[24:36, :], links[36:48, :]]
+        g1.append(jnp.dot(total.astype(bf16), tight80, preferred_element_type=f32))
+    g1 = jnp.concatenate(g1, axis=0)
+    g1 = jnp.concatenate([g1, jnp.zeros((288, 74), f32)], axis=1)
+    gm1[0:144, :] = (g1[0:144] + pltpu.roll(g1[144:288], 64, 1)).astype(bf16)
+    bias = jnp.concatenate([bias2, bias1, jnp.zeros((32, 1), f32)], axis=0)
+    lane = lax.broadcasted_iota(jnp.int32, (112, LANES), 1)
+    gm1[144:256, :] = jnp.where(lane == 0, bias, 0.0).astype(bf16)
+    rows1 = 256 // nt
+    copies_e = to_others(
+        "ta", lambda peer: gm1.at[pl.ds(pl.multiple_of(peer * rows1, 16), rows1)],
+        lambda k: got_e.at[k], send_e, recv_e,
+    )
+
+    x_two = [lk[0:12, :], lk[12:24, :]]
+    y_two = [lk[24:36, :], lk[36:48, :]]
     pairs = [[sin_cos(psi) for psi in three] for three in loop_phases(x_two, y_two)]
+
+    total = mid_b[mz]
+    for k, copy in enumerate(copies_b):
+        copy.wait()
+        total = total + got_b[k + 1]
+    part_c[...] = total
+    copies_c = to_others("gz", lambda peer: part_c, lambda k: all_c.at[mz], send_c, recv_c)
+    all_c[mz] = total
 
     phase_copy.wait()
     for copy in preact_copies:
@@ -428,67 +533,56 @@
         out_link[24 + c * 12 : 36 + c * 12, :] = y_ctx
         out_link[48 + c * 12 : 60 + c * 12, :] = cot[c * 12 : c * 12 + 12, :] - grad + shifted(grad, 0, -1)
 
-
-def sum_kernel(scale, grad, out, got1, mid, got2, fin, send1, recv1, send2, recv2, send3, recv3):
-    nt, nz = lax.axis_size("ta"), lax.axis_size("gz")
-    mt, mz = lax.axis_index("ta"), lax.axis_index("gz")
-    rows = grad.shape[0] // nt
-    barrier = pltpu.get_barrier_semaphore()
-    for k in range(1, nt):
-        pl.semaphore_signal(barrier, inc=1, device_id=(lax.rem(mt + k, nt), mz), device_id_type=MESH_ID)
+    total = gm1[pl.ds(pl.multiple_of(mt * rows1, 16), rows1), :].astype(f32)
+    for k, copy in enumerate(copies_e):
+        copy.wait()
+        total = total + got_e[k + 1].astype(f32)
+    mid_f[...] = (total * scale).astype(bf16)
+    copies_f = to_others("gz", lambda peer: mid_f, lambda k: got_f.at[mz], send_f, recv_f)
+    got_f[mz] = mid_f[...]
+
+    for copy in copies_c:
+        copy.wait()
+    fin_d[...] = jnp.concatenate([all_c[p] for p in range(nz)], axis=0).astype(bf16)
+    mine2 = pl.ds(pl.multiple_of(mt * rows2, 16), rows2)
+    copies_d = to_others("ta", lambda peer: fin_d, lambda k: out2.at[mine2], send_d, recv_d)
+    out2[mine2, :] = fin_d[...]
+
+    for copy in copies_f:
+        copy.wait()
+    total = got_f[0].astype(f32)
     for k in range(1, nz):
-        pl.semaphore_signal(barrier, inc=1, device_id=(mt, lax.rem(mz + k, nz)), device_id_type=MESH_ID)
-    pl.semaphore_wait(barrier, nt + nz - 2)
-
-    copies = []
-    for k in range(1, nt):
-        peer = lax.rem(mt + k, nt)
-        copy = pltpu.make_async_remote_copy(
-            src_ref=grad.at[pl.ds(pl.multiple_of(peer * rows, 16), rows)],
-            dst_ref=got1.at[k],
-            send_sem=send1.at[k], recv_sem=recv1.at[k],
-            device_id=(peer, mz), device_id_type=MESH_ID,
-        )
-        copy.start()
-        copies.append(copy)
-    total = grad[pl.ds(pl.multiple_of(mt * rows, 16), rows), :].astype(f32)
-    for k, copy in enumerate(copies):
-        copy.wait()
-        total = total + got1[k + 1].astype(f32)
-    mid[...] = (total * scale).astype(bf16)
-
-    copies = []
-    for k in range(1, nz):
-        peer = lax.rem(mz + k, nz)
-        copy = pltpu.make_async_remote_copy(
-            src_ref=mid, dst_ref=got2.at[mz],
-            send_sem=send2.at[k], recv_sem=recv2.at[k],
-            device_id=(mt, peer), device_id_type=MESH_ID,
-        )
-        copy.start()
-        copies.append(copy)
-    got2[mz] = mid[...]
-    for copy in copies:
-        copy.wait()
-    total = got2[0].astype(f32)
-    for k in range(1, nz):
-        total = total + got2[k].astype(f32)
-    fin[...] = total.astype(bf16)
-
-    copies = []
-    mine = pl.ds(pl.multiple_of(mt * rows, 16), rows)
-    for k in range(1, nt):
-        peer = lax.rem(mt + k, nt)
-        copy = pltpu.make_async_remote_copy(
-            src_ref=fin, dst_ref=out.at[mine],
-            send_sem=send3.at[k], recv_sem=recv3.at[k],
-            device_id=(peer, mz), device_id_type=MESH_ID,
-        )
-        copy.start()
-        copies.append(copy)
-    out[mine, :] = fin[...]
-    for copy in copies:
-        copy.wait()
+        total = total + got_f[k].astype(f32)
+    fin_g[...] = total.astype(bf16)
+    mine1 = pl.ds(pl.multiple_of(mt * rows1, 16), rows1)
+    copies_h = to_others("ta", lambda peer: fin_g, lambda k: out1.at[mine1], send_h, recv_h)
+    out1[mine1, :] = fin_g[...]
+    for copy in copies_d:
+        copy.wait()
+    for copy in copies_h:
+        copy.wait()
+
+
+def write_kernel(link, sum2, sum1, out_link, out_first, out_bias1, out_second, out_bias2):
+    for d in range(3):
+        for c in range(2):
+            for t in range(LT):
+                out_link[d, c, t] = link[pl.ds(d * 24 + c * 12 + t * 4, LZ), :]
+    out_second[:, 0:128] = sum2[0:432, :].astype(f32)
+    out_second[:, 128:256] = sum2[432:864, :].astype(f32)
+    tail = sum2[864:976, :].astype(f32)
+    for g in range(4):
+        count = min(112, 432 - g * 112)
+        out_second[g * 112 : g * 112 + count, 256:288] = rolled(tail, -32 * g)[0:count, 0:32]
+    half = sum1[0:144, :].astype(f32)
+    out_first[0:144, :] = half[:, 0:54]
+    out_first[144:288, :] = pltpu.roll(half, 64, 1)[:, 0:54]
+    for out, begin, count in ((out_bias2, 144, OUTC), (out_bias1, 192, HID)):
+        col = sum1[begin : begin + count, :].astype(f32)[:, 0:1]
+        eye = lax.broadcasted_iota(jnp.int32, (count, count), 0) == lax.broadcasted_iota(
+            jnp.int32, (count, count), 1
+        )
+        out[...] = jnp.sum(jnp.where(eye, col, 0.0), axis=0, keepdims=True)
 
 
 def vmem():
@@ -500,77 +594,91 @@
     second_weight, second_bias, cotangent, logdet_cotangent,
 ):
     nt, nz = lax.axis_size("ta"), lax.axis_size("gz")
-    fw = first_weight.reshape(3, 3, HID, 9, 6)
-    fw = jnp.pad(fw, ((0, 0), (0, 0), (0, 0), (0, 0), (0, 2))).reshape(3, 96, 72)
-    wt1 = fw.reshape(288, 72).T
-    w1p = jnp.pad(fw, ((0, 0), (0, 0), (0, 8))).transpose(1, 0, 2).reshape(96, 240)
-    w2k = second_weight.reshape(3, 144, 288).transpose(1, 0, 2).reshape(144, 864)
-    wt2 = second_weight.reshape(432, 288).T
-
     dma = pltpu.SemaphoreType.DMA
-    out_link, out_grad = pl.pallas_call(
-        main_kernel,
+    mem = pltpu.VMEM
+    rows2, rows1 = 1024 // nt, 256 // nt
+    part = rows2 // nz
+    scale = 1.0 / math.sqrt(nt * nz * PLANES * LANES)
+    link, sum2, sum1 = pl.pallas_call(
+        functools.partial(main_kernel, scale),
         out_shape=(
             jax.ShapeDtypeStruct((72, LANES), f32),
-            jax.ShapeDtypeStruct((512, 384), bf16),
+            jax.ShapeDtypeStruct((1024, LANES), bf16),
+            jax.ShapeDtypeStruct((256, LANES), bf16),
         ),
-        in_specs=[vmem()] * 11,
-        out_specs=(vmem(), vmem()),
+        in_specs=[vmem()] * 9,
+        out_specs=(vmem(), vmem(), vmem()),
         scratch_shapes=[
-            pltpu.VMEM((7, 32, LANES), f32),
-            pltpu.VMEM((64, LANES), f32),
-            pltpu.VMEM((560, 1024), bf16),
-            pltpu.VMEM((5, HID, 512), f32),
-            pltpu.VMEM((1440, 768), bf16),
-            pltpu.VMEM((LT, OUTC, 512), f32),
-            pltpu.VMEM((7, 32, LANES), f32),
-            pltpu.VMEM((7, 32, LANES), f32),
-            pltpu.VMEM((16, LANES), f32),
-            pltpu.VMEM((8, LANES), f32),
-            pltpu.VMEM((8, LANES), f32),
-            pltpu.VMEM((2, 16, LANES), f32),
-            pltpu.VMEM((5, 6, OUTC, LANES), bf16),
-            pltpu.VMEM((5, 6, HID, LANES), bf16),
-            pltpu.VMEM((96, LANES), f32),
-            pltpu.VMEM((432, LANES), f32),
+            mem((72, LANES), f32),
+            mem((24, LANES), jnp.int32),
+            mem((24, LANES), f32),
+            mem((2, 16, LANES), f32),
+            mem((96, 240), bf16),
+            mem((144, 864), bf16),
+            mem((288, 432), bf16),
+            mem((72, 288), bf16),
+            mem((7, 32, LANES), f32),
+            mem((64, LANES), f32),
+            mem((560, 1024), bf16),
+            mem((5, HID, 512), f32),
+            mem((1440, 768), bf16),
+            mem((LT, OUTC, 512), f32),
+            mem((7, 32, LANES), f32),
+            mem((7, 32, LANES), f32),
+            mem((16, LANES), f32),
+            mem((8, LANES), f32),
+            mem((8, LANES), f32),
+            mem((2, 16, LANES), f32),
+            mem((5, 6, OUTC, LANES), bf16),
+            mem((5, 6, HID, LANES), bf16),
+            mem((96, LANES), f32),
+            mem((448, LANES), f32),
+            mem((1024, LANES), bf16),
+            mem((nt, rows2, LANES), bf16),
+            mem((nz, part, LANES), f32),
+            mem((nz, part, LANES), f32),
+            mem((part, LANES), f32),
+            mem((nz, part, LANES), f32),
+            mem((rows2, LANES), bf16),
+            mem((256, LANES), bf16),
+            mem((nt, rows1, LANES), bf16),
+            mem((rows1, LANES), bf16),
+            mem((nz, rows1, LANES), bf16),
+            mem((rows1, LANES), bf16),
             dma((8,)), dma((8,)), dma((8,)), dma((8,)), dma((8,)), dma((8,)), dma, dma,
+            dma((nt,)), dma((nt,)), dma((nz,)), dma((nz,)), dma((nz,)), dma((nz,)), dma((nt,)), dma((nt,)),
+            dma((nt,)), dma((nt,)), dma((nz,)), dma((nz,)), dma((nt,)), dma((nt,)),
         ],
         compiler_params=pltpu.CompilerParams(
             collective_id=0, has_side_effects=True, vmem_limit_bytes=40 * 1024 * 1024
         ),
         name="main_kernel",
     )(
-        link_phases.reshape(72, LANES),
-        active.reshape(PLANES, LANES),
-        bin_index.reshape(2 * PLANES, LANES),
-        w1p, first_bias.reshape(HID, 1), w2k, second_bias.reshape(OUTC, 1), wt2, wt1,
-        cotangent.reshape(2 * PLANES, LANES),
-        logdet_cotangent.reshape(PLANES, LANES),
-    )
-
-    rows = 512 // nt
-    scale = 1.0 / math.sqrt(nt * nz * PLANES * LANES)
-    summed = pl.pallas_call(
-        functools.partial(sum_kernel, scale),
-        out_shape=jax.ShapeDtypeStruct((512, 384), bf16),
-        in_specs=[vmem()],
-        out_specs=vmem(),
-        scratch_shapes=[
-            pltpu.VMEM((nt, rows, 384), bf16),
-            pltpu.VMEM((rows, 384), bf16),
-            pltpu.VMEM((nz, rows, 384), bf16),
-            pltpu.VMEM((rows, 384), bf16),
-            dma((nt,)), dma((nt,)), dma((nz,)), dma((nz,)), dma((nt,)), dma((nt,)),
-        ],
-        compiler_params=pltpu.CompilerParams(
-            collective_id=1, has_side_effects=True, vmem_limit_bytes=40 * 1024 * 1024
+        link_phases, active, bin_index,
+        first_weight.reshape(288, 54), first_bias.reshape(1, HID),
+        second_weight.reshape(432, 288), second_bias.reshape(1, OUTC),
+        cotangent, logdet_cotangent,
+    )
+    link_grad, first, bias1, second, bias2 = pl.pallas_call(
+        write_kernel,
+        out_shape=(
+            jax.ShapeDtypeStruct((3, 2, LT, LZ, LANES), f32),
+            jax.ShapeDtypeStruct((288, 54), f32),
+            jax.ShapeDtypeStruct((1, HID), f32),
+            jax.ShapeDtypeStruct((432, 288), f32),
+            jax.ShapeDtypeStruct((1, OUTC), f32),
         ),
-        name="sum_kernel",
-    )(out_grad)
-    second = summed[0:432, 0:288].astype(f32).reshape(9, OUTC, 288)
-    first = summed[0:288, 304:376].astype(f32).reshape(9, HID, 9, 8)[..., 0:6].reshape(9, HID, 54)
-    bias = summed[0:80, 288].astype(f32)
-    return (out_link.reshape(3, 2, LT, LZ, LANES), first, bias[48:80], second, bias[0:48])
+        in_specs=[vmem()] * 3,
+        out_specs=(vmem(),) * 5,
+        name="write_kernel",
+    )(link, sum2, sum1)
+    return (
+        link_grad,
+        first.reshape(9, HID, 54),
+        bias1.reshape(HID),
+        second.reshape(9, OUTC, 288),
+        bias2.reshape(OUTC),
+    )
 
 
 def solution(mesh):

time: 73.9 us -> 59.3 us (0.80)
  Pallas kernels: 63.1 us -> 50.8 us
  local copies, waits for them, and re-layouts: 8.67 us -> 7.32 us
  other arithmetic: 1 us -> 0 us
    pallas_call x2, Pallas kernels: 63.1 us -> 50.8 us  [the longest x1 48.9 us: local(): pl.pallas_call(functools.partial(main_kernel, scale), out_shape=(jax.Shap...]
    unnamed x13 -> x24, local copies, waits for them, and re-layouts: 2.77 us -> 7.32 us
    reshape x12 -> x0, local copies, waits for them, and re-layouts: 4.02 us -> none  [the longest x1 0.74 us: local(): second_bias.reshape(OUTC, 1)]
    slice x6 -> x0, local copies, waits for them, and re-layouts: 1.49 us -> none  [the longest x1 0.63 us: local(): bias[0:48]]
    reshape x2 -> x0, other arithmetic: 0.92 us -> none  [the longest x1 0.88 us: local(): second = summed[0:432, 0:288].astype(f32).reshape(9, OUTC, 288)]
where the time goes in v1:
time: 59.3 us; the launch traced here: 58.9 us
  Pallas kernels  50.8 us (86%)
  local copies, waits for them, and re-layouts  7.32 us (12%)
  between operations  0.68 us (1%)
    pallas_call x1, Pallas kernels, local(): pl.pallas_call(functools.partial(main_kernel, scale), out_shape=(jax.Shap...  48.9 us
    unnamed x24, local copies, waits for them, and re-layouts  7.32 us
    pallas_call x1, Pallas kernels, local(): pl.pallas_call(write_kernel, out_shape=(jax.ShapeDtypeStruct((3, 2, LT, L...  1.93 us

profile of v1, /device:TPU:1, one launch (start us, length us, event | category | flops | bytes accessed | tf_op | source)
XLA Modules:
  0.0 58.9 jit_solution(3780576888154329056)
XLA Ops:
  0.6 0.0 copy-start.8
  0.6 0.0 copy-start.10
  0.7 0.0 copy-start.11
  0.7 0.7 %copy-done.8 = s32[3,4,128]{2,1,0:T(4,128)S(1)} copy-done((s32[3,4,128]{2,1,0:T(4,128)S(1)}, s32[3,4,128]{2,1,0:T(4,128)}, u32[]{:S(2)}) %copy-start.8) | copy-done | bytes 6168
  1.3 0.0 copy-done.10
  1.3 0.0 copy-done.11
  1.3 0.0 copy-start
  1.3 1.0 %copy-done = bf16[9,48,288]{2,1,0:T(8,128)(2,1)S(1)} copy-done((bf16[9,48,288]{2,1,0:T(8,128)(2,1)S(1)}, bf16[9,48,288]{2,1,0:T(8,128)(2,1)}, u32[]{:S(2)}) %copy-start) | copy-done | bytes 248856
  2.3 0.0 copy-start.2
  2.3 0.9 %copy-done.2 = bf16[9,32,54]{2,1,0:T(8,128)(2,1)S(1)} copy-done((bf16[9,32,54]{2,1,0:T(8,128)(2,1)S(1)}, bf16[9,32,54]{2,1,0:T(8,128)(2,1)}, u32[]{:S(2)}) %copy-start.2) | copy-done | bytes 31128
  3.2 0.0 copy-start.5
  3.2 0.8 %copy-done.5 = f32[3,2,3,4,128]{4,3,2,1,0:T(4,128)S(1)} copy-done((f32[3,2,3,4,128]{4,3,2,1,0:T(4,128)S(1)}, f32[3,2,3,4,128]{4,3,2,1,0:T(4,128)}, u32[]{:S(2)}) %copy-start.5) | copy-done | bytes 36888
  4.0 0.0 copy-start.6
  4.0 0.7 %copy-done.6 = s32[2,3,4,128]{3,2,1,0:T(4,128)S(1)} copy-done((s32[2,3,4,128]{3,2,1,0:T(4,128)S(1)}, s32[2,3,4,128]{3,2,1,0:T(4,128)}, u32[]{:S(2)}) %copy-start.6) | copy-done | bytes 12312
  4.7 0.0 copy-start.7
  4.7 0.7 %copy-done.7 = f32[2,3,4,128]{3,2,1,0:T(4,128)S(1)} copy-done((f32[2,3,4,128]{3,2,1,0:T(4,128)S(1)}, f32[2,3,4,128]{3,2,1,0:T(4,128)}, u32[]{:S(2)}) %copy-start.7) | copy-done | bytes 12312
  5.4 0.0 copy-start.9
  5.4 0.7 %copy-done.9 = f32[3,4,128]{2,1,0:T(4,128)S(1)} copy-done((f32[3,4,128]{2,1,0:T(4,128)S(1)}, f32[3,4,128]{2,1,0:T(4,128)}, u32[]{:S(2)}) %copy-start.9) | copy-done | bytes 6168
  6.1 48.9 %main_kernel.1 = (f32[72,128]{1,0:T(8,128)S(1)}, bf16[1024,128]{1,0:T(8,128)(2,1)S(1)}, bf16[256,128]{1,0:T(8,128)(2,1)S(1)}) custom-call(f32[3,2,3,4,128]{4,3,2,1,0:T(4,128)S(1)} %copy-done.5, s32[3,4,128]{2,1,0:T(4,128)S(1)} %copy-done.8, s32[2,3,4,128]{3,2,1,0:T(4,128)S(1)} %copy-done.6, bf16[288,54]{1,0:T(8,128)(2,1)S(1)} %bitcast.9, ...), custom_call_target="tpu_custom_call" | custom-call | tf_op jit(solution)/shard_map/main_kernel/pallas_call | solution.py:602
  55.0 0.0 copy-start.1
  55.0 0.7 %copy-done.1 = bf16[1024,128]{1,0:T(8,128)(2,1)} copy-done((bf16[1024,128]{1,0:T(8,128)(2,1)}, bf16[1024,128]{1,0:T(8,128)(2,1)S(1)}, u32[]{:S(2)}) %copy-start.1) | copy-done | bytes 262168
  55.7 0.0 copy-start.3
  55.7 0.6 %copy-done.3 = bf16[256,128]{1,0:T(8,128)(2,1)} copy-done((bf16[256,128]{1,0:T(8,128)(2,1)}, bf16[256,128]{1,0:T(8,128)(2,1)S(1)}, u32[]{:S(2)}) %copy-start.3) | copy-done | bytes 65560
  56.3 0.0 copy-start.4
  56.3 0.6 %copy-done.4 = f32[72,128]{1,0:T(8,128)} copy-done((f32[72,128]{1,0:T(8,128)}, f32[72,128]{1,0:T(8,128)S(1)}, u32[]{:S(2)}) %copy-start.4) | copy-done | bytes 36888
  56.9 1.9 %write_kernel.1 = (f32[3,2,3,4,128]{4,3,2,1,0:T(4,128)}, f32[288,54]{1,0:T(8,128)}, f32[1,32]{1,0:T(1,128)}, f32[432,288]{1,0:T(8,128)}, f32[1,48]{1,0:T(1,128)}) custom-call(f32[72,128]{1,0:T(8,128)} %copy-done.4, bf16[1024,128]{1,0:T(8,128)(2,1)} %copy-done.1, bf16[256,128]{1,0:T(8,128)(2,1)} %copy-done.3), custom_call_target="tpu_custom_call" | custom-call | tf_op jit(solution)/shard_map/write_kernel/pallas_call | solution.py:662
Async XLA Ops:
  0.6 0.7 %copy-start.8 = (s32[3,4,128]{2,1,0:T(4,128)S(1)}, s32[3,4,128]{2,1,0:T(4,128)}, u32[]{:S(2)}) copy-start(s32[3,4,128]{2,1,0:T(4,128)} %act.1) | copy-start | bytes 18436
  0.6 0.7 %copy-start.10 = (f32[32]{0:T(128)S(1)}, f32[32]{0:T(128)}, u32[]{:S(2)}) copy-start(f32[32]{0:T(128)} %param.13) | copy-start | bytes 388
  0.7 0.7 %copy-start.11 = (f32[48]{0:T(128)S(1)}, f32[48]{0:T(128)}, u32[]{:S(2)}) copy-start(f32[48]{0:T(128)} %param.15) | copy-start | bytes 580
  1.3 1.0 %copy-start = (bf16[9,48,288]{2,1,0:T(8,128)(2,1)S(1)}, bf16[9,48,288]{2,1,0:T(8,128)(2,1)}, u32[]{:S(2)}) copy-start(bf16[9,48,288]{2,1,0:T(8,128)(2,1)} %param.14) | copy-start | bytes 746500
  2.3 0.9 %copy-start.2 = (bf16[9,32,54]{2,1,0:T(8,128)(2,1)S(1)}, bf16[9,32,54]{2,1,0:T(8,128)(2,1)}, u32[]{:S(2)}) copy-start(bf16[9,32,54]{2,1,0:T(8,128)(2,1)} %param.12) | copy-start | bytes 93316
  3.2 0.8 %copy-start.5 = (f32[3,2,3,4,128]{4,3,2,1,0:T(4,128)S(1)}, f32[3,2,3,4,128]{4,3,2,1,0:T(4,128)}, u32[]{:S(2)}) copy-start(f32[3,2,3,4,128]{4,3,2,1,0:T(4,128)} %links.1) | copy-start | bytes 110596
  4.0 0.7 %copy-start.6 = (s32[2,3,4,128]{3,2,1,0:T(4,128)S(1)}, s32[2,3,4,128]{3,2,1,0:T(4,128)}, u32[]{:S(2)}) copy-start(s32[2,3,4,128]{3,2,1,0:T(4,128)} %bins_in.1) | copy-start | bytes 36868
  4.7 0.7 %copy-start.7 = (f32[2,3,4,128]{3,2,1,0:T(4,128)S(1)}, f32[2,3,4,128]{3,2,1,0:T(4,128)}, u32[]{:S(2)}) copy-start(f32[2,3,4,128]{3,2,1,0:T(4,128)} %cot_in.1) | copy-start | bytes 36868
  5.4 0.7 %copy-start.9 = (f32[3,4,128]{2,1,0:T(4,128)S(1)}, f32[3,4,128]{2,1,0:T(4,128)}, u32[]{:S(2)}) copy-start(f32[3,4,128]{2,1,0:T(4,128)} %ldc_in.1) | copy-start | bytes 18436
  55.0 0.7 %copy-start.1 = (bf16[1024,128]{1,0:T(8,128)(2,1)}, bf16[1024,128]{1,0:T(8,128)(2,1)S(1)}, u32[]{:S(2)}) copy-start(bf16[1024,128]{1,0:T(8,128)(2,1)S(1)} %get-tuple-element.14.sum2) | copy-start | bytes 786436
  55.7 0.6 %copy-start.3 = (bf16[256,128]{1,0:T(8,128)(2,1)}, bf16[256,128]{1,0:T(8,128)(2,1)S(1)}, u32[]{:S(2)}) copy-start(bf16[256,128]{1,0:T(8,128)(2,1)S(1)} %get-tuple-element.15.sum1) | copy-start | bytes 196612
  56.3 0.6 %copy-start.4 = (f32[72,128]{1,0:T(8,128)}, f32[72,128]{1,0:T(8,128)S(1)}, u32[]{:S(2)}) copy-start(f32[72,128]{1,0:T(8,128)S(1)} %get-tuple-element.13.link) | copy-start | bytes 110596

commit v2 on v1

--- a/solution.py
+++ b/solution.py
@@ -108,41 +108,70 @@
 
 
 def main_kernel(
-    scale, links, act, bins_in, first_w, b1, second_w, b2, cot_in, ldc_in,
-    out_link, out2, out1,
-    lk, bins, cot, site, w1p, w2k, wt2, wt1,
-    lbuf, fs, fcols, pres, cols, sigs, red, coef, xab, pgs, pgr, pgv,
-    pbuf, qbuf, fgs, tails, gm2, got_a, mid_b, got_b, part_c, all_c, fin_d,
-    gm1, got_e, mid_f, got_f, fin_g,
-    send_l, recv_l, send_p, recv_p, send_q, recv_q, send_g, recv_g,
-    send_a, recv_a, send_b, recv_b, send_c, recv_c, send_d, recv_d,
-    send_e, recv_e, send_f, recv_f, send_h, recv_h,
+    scale, *refs
 ):
+    given, refs = refs[:9], refs[9:]
+    (out_link, out2, out1), refs = refs[:3], refs[3:]
+    held, refs = refs[:9], refs[9:]
+    links, act, bins_in, first_w, b1, second_w, b2, cot_in, ldc_in = held
+    (
+        lk, bins, cot, site, w1p, w2k, wt2, wt1,
+        lbuf, fs, fcols, pres, cols, sigs, red, coef, xab, pgs, pgr, pgv,
+        pbuf, qbuf, fgs, tails, gm2, got_a, mid_b, got_b, fin_d,
+        gm1, got_e, mid_f, got_f, fin_g, link_out,
+        in_sem, out_sem, send_l, recv_l, send_p, recv_p, send_q, recv_q, send_g, recv_g,
+        send_a, recv_a, send_b, recv_b, send_d, recv_d,
+        send_e, recv_e, send_f, recv_f, send_h, recv_h,
+    ) = refs
+    loads = [pltpu.make_async_copy(src, dst, in_sem.at[i]) for i, (src, dst) in enumerate(zip(given, held))]
+    for load in loads:
+        load.start()
+
     nt, nz = lax.axis_size("ta"), lax.axis_size("gz")
     mt, mz = lax.axis_index("ta"), lax.axis_index("gz")
+    nx, nd = 2 * nt, nz // 2
+    side, deep = lax.rem(mz, 2), mz // 2
+    mx = 2 * mt + side
+
+    def wide_peer(k):
+        return (lax.rem(mt + k // 2, nt), mz + (k % 2) * (1 - 2 * side))
+
+    def deep_peer(k):
+        return (mt, lax.rem(mz + 2 * k, nz))
+
+    wide_order = list(range(1, nx))
+    deep_order = sorted(range(1, nd), key=lambda k: -min(k, nd - k))
     barrier = pltpu.get_barrier_semaphore()
-    corners = [(dt, dz) for dt, dz in DIRS if dt != 0 and dz != 0]
-    for dt, dz in corners:
-        pl.semaphore_signal(barrier, inc=1, device_id=neighbour(dt, dz), device_id_type=MESH_ID)
-    for k in range(1, nt):
-        pl.semaphore_signal(barrier, inc=1, device_id=(lax.rem(mt + k, nt), mz), device_id_type=MESH_ID)
-    for k in range(1, nz):
-        pl.semaphore_signal(barrier, inc=1, device_id=(mt, lax.rem(mz + k, nz)), device_id_type=MESH_ID)
-
-    def to_others(axis, src, dst, send, recv):
-        count, me = (nt, mt) if axis == "ta" else (nz, mz)
+    cross = lax.rem(mz - 1 + 2 * side + nz, nz)
+    greeted = [(lax.rem(mt + dt + nt, nt), cross) for dt in (-1, 0, 1)]
+    greeted += [wide_peer(k) for k in wide_order] + [deep_peer(k) for k in deep_order]
+    for peer in greeted:
+        pl.semaphore_signal(barrier, inc=1, device_id=peer, device_id_type=MESH_ID)
+
+    def to_wide(src, dst, send, recv):
         copies = []
-        for k in range(1, count):
-            peer = lax.rem(me + k, count)
+        for k in wide_order:
+            peer = wide_peer(k)
             copy = pltpu.make_async_remote_copy(
-                src_ref=src(peer), dst_ref=dst(k),
-                send_sem=send.at[k], recv_sem=recv.at[k],
-                device_id=(peer, mz) if axis == "ta" else (mt, peer), device_id_type=MESH_ID,
+                src_ref=src(2 * peer[0] + lax.rem(peer[1], 2)), dst_ref=dst(k),
+                send_sem=send.at[k], recv_sem=recv.at[k], device_id=peer, device_id_type=MESH_ID,
             )
             copy.start()
             copies.append(copy)
         return copies
 
+    def to_deep(src, dst, send, recv):
+        copies = []
+        for k in deep_order:
+            copy = pltpu.make_async_remote_copy(
+                src_ref=src, dst_ref=dst,
+                send_sem=send.at[k], recv_sem=recv.at[k], device_id=deep_peer(k), device_id_type=MESH_ID,
+            )
+            copy.start()
+            copies.append(copy)
+        return copies
+
+    loads[0].wait()
     for d in range(3):
         for c in range(2):
             for t in range(LT):
@@ -150,7 +179,7 @@
     for comp in range(4):
         for t in range(LT):
             lbuf[2 + t, pl.ds(8 + comp, LZ, stride=4), :] = lk[pl.ds(comp * PLANES + t * LZ, LZ), :]
-    pl.semaphore_wait(barrier, nt + nz - 2 + len(corners))
+    pl.semaphore_wait(barrier, len(greeted))
 
     t_from = {-1: slice(2, 4), 0: slice(2, 5), 1: slice(3, 5)}
     t_into = {-1: slice(5, 7), 0: slice(2, 5), 1: slice(0, 2)}
@@ -168,6 +197,8 @@
         link_copies.append(copy)
     fs[...] = jnp.zeros_like(fs)
 
+    for load in loads[1:]:
+        load.wait()
     for t in range(LT):
         site[0, pl.ds(t * LZ, LZ), :] = act[t].astype(f32)
         site[1, pl.ds(t * LZ, LZ), :] = ldc_in[t]
@@ -190,9 +221,6 @@
             for i in range(3)
         ],
         axis=1,
-    ).astype(bf16)
-    wt1[...] = lax.dot_general(
-        one_hot(72, 0), first_w[...], nt_dims, preferred_element_type=f32
     ).astype(bf16)
     w2k[...] = jnp.concatenate(
         [second_w[i * 144 : (i + 1) * 144, :].astype(f32) for i in range(3)], axis=1
@@ -226,7 +254,7 @@
             fcols[pl.ds(row, 80), z * LANES : (z + 1) * LANES] = jnp.concatenate(blocks, axis=0).astype(bf16)
         return carry
 
-    lax.fori_loop(0, 7, feature_slice, 0)
+    lax.fori_loop(0, 7, feature_slice, 0, unroll=True)
 
     def hidden_slice(t, carry):
         got = jnp.dot(
@@ -241,7 +269,7 @@
             cols[pl.ds(row, 288), z * LANES : (z + 1) * LANES] = jnp.concatenate(blocks, axis=0).astype(bf16)
         return carry
 
-    lax.fori_loop(0, 5, hidden_slice, 0)
+    lax.fori_loop(0, 5, hidden_slice, 0, unroll=True)
 
     level = lax.broadcasted_iota(jnp.int32, (K, LANES), 0)
 
@@ -271,7 +299,7 @@
                     red[q, pl.ds(c * 16 + plane, 1), :] = jnp.sum(value, axis=0, keepdims=True)
         return carry
 
-    lax.fori_loop(0, LT, param_slice, 0)
+    lax.fori_loop(0, LT, param_slice, 0, unroll=True)
 
     live = site[0, 0:12, :]
     g_log = live * site[1, 0:12, :]
@@ -351,7 +379,7 @@
         return total
 
     bias2 = jnp.sum(
-        lax.fori_loop(0, LT, param_grad_slice, jnp.zeros((OUTC, LANES), f32)), axis=1, keepdims=True
+        lax.fori_loop(0, LT, param_grad_slice, jnp.zeros((OUTC, LANES), f32), unroll=True), axis=1, keepdims=True
     )
 
     h_from = {-1: slice(1, 2), 0: slice(1, 4), 1: slice(3, 4)}
@@ -407,11 +435,13 @@
     gm2[864:976, :] = tail.astype(bf16)
     gm2[976:1024, :] = jnp.zeros((48, LANES), bf16)
 
-    rows2 = 1024 // nt
-    rows_part = rows2 // nz
-    copies_a = to_others(
-        "ta", lambda peer: gm2.at[pl.ds(pl.multiple_of(peer * rows2, 16), rows2)],
-        lambda k: got_a.at[k], send_a, recv_a,
+    rows2, rows1 = 1024 // nx, 256 // nx
+
+    def wide_rows(index, rows):
+        return pl.ds(pl.multiple_of(index * rows, rows), rows)
+
+    copies_a = to_wide(
+        lambda index: gm2.at[wide_rows(index, rows2)], lambda k: got_a.at[k], send_a, recv_a
     )
 
     for copy in param_copies:
@@ -437,19 +467,10 @@
         return total
 
     bias1 = jnp.sum(
-        lax.fori_loop(0, LT, hidden_grad_slice, jnp.zeros((HID, LANES), f32)), axis=1, keepdims=True
+        lax.fori_loop(0, LT, hidden_grad_slice, jnp.zeros((HID, LANES), f32), unroll=True), axis=1, keepdims=True
     )
 
     preact_copies = send_halo(qbuf, send_q, recv_q)
-
-    total = gm2[pl.ds(pl.multiple_of(mt * rows2, 16), rows2), :].astype(f32)
-    for k, copy in enumerate(copies_a):
-        copy.wait()
-        total = total + got_a[k + 1].astype(f32)
-    total = total * scale
-    for p in range(nz):
-        mid_b[p] = total[p * rows_part : (p + 1) * rows_part, :]
-    copies_b = to_others("gz", lambda peer: mid_b.at[peer], lambda k: got_b.at[k], send_b, recv_b)
 
     tight80 = one_hot(80, 0)
     spread_q = [spread(qbuf, t, HID) for t in range(LT)]
@@ -465,27 +486,21 @@
         g1.append(jnp.dot(total.astype(bf16), tight80, preferred_element_type=f32))
     g1 = jnp.concatenate(g1, axis=0)
     g1 = jnp.concatenate([g1, jnp.zeros((288, 74), f32)], axis=1)
-    gm1[0:144, :] = (g1[0:144] + pltpu.roll(g1[144:288], 64, 1)).astype(bf16)
+    gm1[0:144, :] = g1[0:144] + pltpu.roll(g1[144:288], 64, 1)
     bias = jnp.concatenate([bias2, bias1, jnp.zeros((32, 1), f32)], axis=0)
     lane = lax.broadcasted_iota(jnp.int32, (112, LANES), 1)
-    gm1[144:256, :] = jnp.where(lane == 0, bias, 0.0).astype(bf16)
-    rows1 = 256 // nt
-    copies_e = to_others(
-        "ta", lambda peer: gm1.at[pl.ds(pl.multiple_of(peer * rows1, 16), rows1)],
-        lambda k: got_e.at[k], send_e, recv_e,
-    )
+    gm1[144:256, :] = jnp.where(lane == 0, bias, 0.0)
+    copies_e = to_wide(
+        lambda index: gm1.at[wide_rows(index, rows1)], lambda k: got_e.at[k], send_e, recv_e
+    )
+
+    wt1[...] = lax.dot_general(
+        one_hot(72, 0), first_w[...], nt_dims, preferred_element_type=f32
+    ).astype(bf16)
 
     x_two = [lk[0:12, :], lk[12:24, :]]
     y_two = [lk[24:36, :], lk[36:48, :]]
     pairs = [[sin_cos(psi) for psi in three] for three in loop_phases(x_two, y_two)]
-
-    total = mid_b[mz]
-    for k, copy in enumerate(copies_b):
-        copy.wait()
-        total = total + got_b[k + 1]
-    part_c[...] = total
-    copies_c = to_others("gz", lambda peer: part_c, lambda k: all_c.at[mz], send_c, recv_c)
-    all_c[mz] = total
 
     phase_copy.wait()
     for copy in preact_copies:
@@ -499,7 +514,30 @@
             fgs[pl.ds(pl.multiple_of((t * LZ + z) * 8, 8), 8), :] = grad
         return carry
 
-    lax.fori_loop(0, LT, feature_grad_slice, 0)
+    lax.fori_loop(0, LT, feature_grad_slice, 0, unroll=True)
+
+    def in_order(parts, count):
+        total = parts[0].astype(f32)
+        for k in range(1, count):
+            total = total + parts[k].astype(f32)
+        return total
+
+    total = gm2[wide_rows(mx, rows2), :].astype(f32)
+    for k, copy in enumerate(copies_a):
+        copy.wait()
+        total = total + got_a[wide_order[k]].astype(f32)
+    mid_b[...] = (total * scale).astype(bf16)
+    copies_b = to_deep(mid_b, got_b.at[deep], send_b, recv_b)
+    got_b[deep] = mid_b[...]
+
+    total = gm1[wide_rows(mx, rows1), :]
+    for k, copy in enumerate(copies_e):
+        copy.wait()
+        total = total + got_e[wide_order[k]]
+    total = total * scale
+    mid_f[...] = total
+    copies_f = to_deep(mid_f, got_f.at[deep], send_f, recv_f)
+    got_f[deep] = total
 
     third = 1.0 / 3.0
     loop_grads = []
@@ -510,7 +548,7 @@
         loop_grads.append((three[0] - three[2], three[1] - three[2]))
     for c in range(2):
         dp, dw, dr = loop_grads[0][c], loop_grads[1][c], loop_grads[2][c]
-        side = dp + dr
+        pair = dp + dr
         x_ctx = (
             dp + dw + dr
             - shifted(dp + dw, -1, 0)
@@ -519,8 +557,8 @@
             - shifted(dr, -2, 0)
         )
         y_ctx = (
-            shifted(side, 0, -1)
-            - side
+            shifted(pair, 0, -1)
+            - pair
             - dw
             + shifted(dw, 0, -2)
             + shifted(dr, -1, -1)
@@ -529,37 +567,27 @@
         pgv[c, 0:4, :] = pgr[c * 4 : c * 4 + 4, :]
         grad = pgv[c, 4:16, :]
         prev = pgv[c, 0:12, :]
-        out_link[c * 12 : c * 12 + 12, :] = grad - prev + x_ctx
-        out_link[24 + c * 12 : 36 + c * 12, :] = y_ctx
-        out_link[48 + c * 12 : 60 + c * 12, :] = cot[c * 12 : c * 12 + 12, :] - grad + shifted(grad, 0, -1)
-
-    total = gm1[pl.ds(pl.multiple_of(mt * rows1, 16), rows1), :].astype(f32)
-    for k, copy in enumerate(copies_e):
+        link_out[c * 12 : c * 12 + 12, :] = grad - prev + x_ctx
+        link_out[24 + c * 12 : 36 + c * 12, :] = y_ctx
+        link_out[48 + c * 12 : 60 + c * 12, :] = cot[c * 12 : c * 12 + 12, :] - grad + shifted(grad, 0, -1)
+
+    stores = [pltpu.make_async_copy(link_out, out_link, out_sem.at[0])]
+    stores[0].start()
+
+    for copy in copies_b:
         copy.wait()
-        total = total + got_e[k + 1].astype(f32)
-    mid_f[...] = (total * scale).astype(bf16)
-    copies_f = to_others("gz", lambda peer: mid_f, lambda k: got_f.at[mz], send_f, recv_f)
-    got_f[mz] = mid_f[...]
-
-    for copy in copies_c:
-        copy.wait()
-    fin_d[...] = jnp.concatenate([all_c[p] for p in range(nz)], axis=0).astype(bf16)
-    mine2 = pl.ds(pl.multiple_of(mt * rows2, 16), rows2)
-    copies_d = to_others("ta", lambda peer: fin_d, lambda k: out2.at[mine2], send_d, recv_d)
-    out2[mine2, :] = fin_d[...]
+    fin_d[...] = in_order(got_b, nd).astype(bf16)
+    copies_d = to_wide(lambda index: fin_d, lambda k: out2.at[wide_rows(mx, rows2)], send_d, recv_d)
+    stores.append(pltpu.make_async_copy(fin_d, out2.at[wide_rows(mx, rows2)], out_sem.at[1]))
+    stores[1].start()
 
     for copy in copies_f:
         copy.wait()
-    total = got_f[0].astype(f32)
-    for k in range(1, nz):
-        total = total + got_f[k].astype(f32)
-    fin_g[...] = total.astype(bf16)
-    mine1 = pl.ds(pl.multiple_of(mt * rows1, 16), rows1)
-    copies_h = to_others("ta", lambda peer: fin_g, lambda k: out1.at[mine1], send_h, recv_h)
-    out1[mine1, :] = fin_g[...]
-    for copy in copies_d:
-        copy.wait()
-    for copy in copies_h:
+    fin_g[...] = in_order(got_f, nd)
+    copies_h = to_wide(lambda index: fin_g, lambda k: out1.at[wide_rows(mx, rows1)], send_h, recv_h)
+    stores.append(pltpu.make_async_copy(fin_g, out1.at[wide_rows(mx, rows1)], out_sem.at[2]))
+    stores[2].start()
+    for copy in copies_d + stores + copies_h:
         copy.wait()
 
 
@@ -574,11 +602,11 @@
     for g in range(4):
         count = min(112, 432 - g * 112)
         out_second[g * 112 : g * 112 + count, 256:288] = rolled(tail, -32 * g)[0:count, 0:32]
-    half = sum1[0:144, :].astype(f32)
+    half = sum1[0:144, :]
     out_first[0:144, :] = half[:, 0:54]
     out_first[144:288, :] = pltpu.roll(half, 64, 1)[:, 0:54]
     for out, begin, count in ((out_bias2, 144, OUTC), (out_bias1, 192, HID)):
-        col = sum1[begin : begin + count, :].astype(f32)[:, 0:1]
+        col = sum1[begin : begin + count, :][:, 0:1]
         eye = lax.broadcasted_iota(jnp.int32, (count, count), 0) == lax.broadcasted_iota(
             jnp.int32, (count, count), 1
         )
@@ -596,19 +624,28 @@
     nt, nz = lax.axis_size("ta"), lax.axis_size("gz")
     dma = pltpu.SemaphoreType.DMA
     mem = pltpu.VMEM
-    rows2, rows1 = 1024 // nt, 256 // nt
-    part = rows2 // nz
+    nx, nd = 2 * nt, nz // 2
+    rows2, rows1 = 1024 // nx, 256 // nx
     scale = 1.0 / math.sqrt(nt * nz * PLANES * LANES)
     link, sum2, sum1 = pl.pallas_call(
         functools.partial(main_kernel, scale),
         out_shape=(
             jax.ShapeDtypeStruct((72, LANES), f32),
             jax.ShapeDtypeStruct((1024, LANES), bf16),
-            jax.ShapeDtypeStruct((256, LANES), bf16),
+            jax.ShapeDtypeStruct((256, LANES), f32),
         ),
-        in_specs=[vmem()] * 9,
-        out_specs=(vmem(), vmem(), vmem()),
+        in_specs=[pl.BlockSpec(memory_space=pltpu.HBM)] * 9,
+        out_specs=(pl.BlockSpec(memory_space=pltpu.HBM),) * 3,
         scratch_shapes=[
+            mem((3, 2, LT, LZ, LANES), f32),
+            mem((LT, LZ, LANES), jnp.int32),
+            mem((2, LT, LZ, LANES), jnp.int32),
+            mem((288, 54), bf16),
+            mem((1, HID), f32),
+            mem((432, 288), bf16),
+            mem((1, OUTC), f32),
+            mem((2, LT, LZ, LANES), f32),
+            mem((LT, LZ, LANES), f32),
             mem((72, LANES), f32),
             mem((24, LANES), jnp.int32),
             mem((24, LANES), f32),
@@ -634,23 +671,22 @@
             mem((96, LANES), f32),
             mem((448, LANES), f32),
             mem((1024, LANES), bf16),
-            mem((nt, rows2, LANES), bf16),
-            mem((nz, part, LANES), f32),
-            mem((nz, part, LANES), f32),
-            mem((part, LANES), f32),
-            mem((nz, part, LANES), f32),
+            mem((nx, rows2, LANES), bf16),
             mem((rows2, LANES), bf16),
-            mem((256, LANES), bf16),
-            mem((nt, rows1, LANES), bf16),
-            mem((rows1, LANES), bf16),
-            mem((nz, rows1, LANES), bf16),
-            mem((rows1, LANES), bf16),
-            dma((8,)), dma((8,)), dma((8,)), dma((8,)), dma((8,)), dma((8,)), dma, dma,
-            dma((nt,)), dma((nt,)), dma((nz,)), dma((nz,)), dma((nz,)), dma((nz,)), dma((nt,)), dma((nt,)),
-            dma((nt,)), dma((nt,)), dma((nz,)), dma((nz,)), dma((nt,)), dma((nt,)),
+            mem((nd, rows2, LANES), bf16),
+            mem((rows2, LANES), bf16),
+            mem((256, LANES), f32),
+            mem((nx, rows1, LANES), f32),
+            mem((rows1, LANES), f32),
+            mem((nd, rows1, LANES), f32),
+            mem((rows1, LANES), f32),
+            mem((72, LANES), f32),
+            dma((9,)), dma((3,)), dma((8,)), dma((8,)), dma((8,)), dma((8,)), dma((8,)), dma((8,)), dma, dma,
+            dma((nx,)), dma((nx,)), dma((nd,)), dma((nd,)), dma((nx,)), dma((nx,)),
+            dma((nx,)), dma((nx,)), dma((nd,)), dma((nd,)), dma((nx,)), dma((nx,)),
         ],
         compiler_params=pltpu.CompilerParams(
-            collective_id=0, has_side_effects=True, vmem_limit_bytes=40 * 1024 * 1024
+            collective_id=0, has_side_effects=True, vmem_limit_bytes=56 * 1024 * 1024
         ),
         name="main_kernel",
     )(
@@ -670,6 +706,7 @@
         ),
         in_specs=[vmem()] * 3,
         out_specs=(vmem(),) * 5,
+        compiler_params=pltpu.CompilerParams(vmem_limit_bytes=56 * 1024 * 1024),
         name="write_kernel",
     )(link, sum2, sum1)
     return (

time: 59.3 us -> 48 us (0.81)
  local copies, waits for them, and re-layouts: 7.32 us -> 0 us
  Pallas kernels: 50.8 us -> 47.2 us
    unnamed x24 -> x0, local copies, waits for them, and re-layouts: 7.32 us -> none
    pallas_call x1, Pallas kernels: 48.9 us -> 45.2 us  [local(): pl.pallas_call(functools.partial(main_kernel, scale), out_shape=(jax.Shap...]
where the time goes in v2:
time: 48 us; the launch traced here: 47.8 us
  Pallas kernels  47.2 us (98%)
  between operations  0.64 us (1%)
    pallas_call x1, Pallas kernels, local(): pl.pallas_call(functools.partial(main_kernel, scale), out_shape=(jax.Shap...  45.2 us
    pallas_call x1, Pallas kernels, local(): pl.pallas_call(write_kernel, out_shape=(jax.ShapeDtypeStruct((3, 2, LT, L...  1.99 us

profile of v2, /device:TPU:1, one launch (start us, length us, event | category | flops | bytes accessed | tf_op | source)
XLA Modules:
  0.0 47.8 jit_solution(5644666740181471952)
XLA Ops:
  0.6 45.2 %main_kernel.1 = (f32[72,128]{1,0:T(8,128)}, bf16[1024,128]{1,0:T(8,128)(2,1)}, f32[256,128]{1,0:T(8,128)}) custom-call(f32[3,2,3,4,128]{4,3,2,1,0:T(4,128)} %refs_0_.1, s32[3,4,128]{2,1,0:T(4,128)} %refs_1_.1, s32[2,3,4,128]{3,2,1,0:T(4,128)} %refs_2_.1, bf16[288,54]{1,0:T(8,128)(2,1)} %bitcast.9, f32[1,32]{1,0:T(1,128)} %bitcast.10, ...), custom_call_target="tpu_custom_call" | custom-call | tf_op jit(solution)/shard_map/main_kernel/pallas_call | solution.py:630
  45.9 2.0 %write_kernel.1 = (f32[3,2,3,4,128]{4,3,2,1,0:T(4,128)}, f32[288,54]{1,0:T(8,128)}, f32[1,32]{1,0:T(1,128)}, f32[432,288]{1,0:T(8,128)}, f32[1,48]{1,0:T(1,128)}) custom-call(f32[72,128]{1,0:T(8,128)} %get-tuple-element.13.link, bf16[1024,128]{1,0:T(8,128)(2,1)} %get-tuple-element.14.sum2, f32[256,128]{1,0:T(8,128)} %get-tuple-element.15.sum1), custom_call_target="tpu_custom_call" | custom-call | tf_op jit(solution)/shard_map/write_kernel/pallas_call | solution.py:698

commit v3 on v2

--- a/solution.py
+++ b/solution.py
@@ -133,13 +133,26 @@
     side, deep = lax.rem(mz, 2), mz // 2
     mx = 2 * mt + side
 
+    flips, weight = [(0, 1 - 2 * side)], 1
+    while weight < nt:
+        flips.append((weight * (1 - 2 * lax.rem(mt // weight, 2)), 0))
+        weight *= 2
+
     def wide_peer(k):
-        return (lax.rem(mt + k // 2, nt), mz + (k % 2) * (1 - 2 * side))
+        along, across = mt, mz
+        for bit, (dt, dz) in enumerate(flips):
+            if k >> bit & 1:
+                along, across = along + dt, across + dz
+        return (along, across)
+
+    def wide_hops(k):
+        steps = (0, 1, 2, 1)
+        return steps[(k >> 2) & 3] + steps[((k >> 4) & 1) * 2 + (k & 1)]
 
     def deep_peer(k):
         return (mt, lax.rem(mz + 2 * k, nz))
 
-    wide_order = list(range(1, nx))
+    wide_order = sorted(range(1, nx), key=lambda k: -wide_hops(k))
     deep_order = sorted(range(1, nd), key=lambda k: -min(k, nd - k))
     barrier = pltpu.get_barrier_semaphore()
     cross = lax.rem(mz - 1 + 2 * side + nz, nz)
@@ -470,8 +483,6 @@
         lax.fori_loop(0, LT, hidden_grad_slice, jnp.zeros((HID, LANES), f32), unroll=True), axis=1, keepdims=True
     )
 
-    preact_copies = send_halo(qbuf, send_q, recv_q)
-
     tight80 = one_hot(80, 0)
     spread_q = [spread(qbuf, t, HID) for t in range(LT)]
     g1 = []
@@ -494,27 +505,7 @@
         lambda index: gm1.at[wide_rows(index, rows1)], lambda k: got_e.at[k], send_e, recv_e
     )
 
-    wt1[...] = lax.dot_general(
-        one_hot(72, 0), first_w[...], nt_dims, preferred_element_type=f32
-    ).astype(bf16)
-
-    x_two = [lk[0:12, :], lk[12:24, :]]
-    y_two = [lk[24:36, :], lk[36:48, :]]
-    pairs = [[sin_cos(psi) for psi in three] for three in loop_phases(x_two, y_two)]
-
-    phase_copy.wait()
-    for copy in preact_copies:
-        copy.wait()
-
-    def feature_grad_slice(t, carry):
-        got = jnp.dot(wt1[...], stacked(qbuf, t), preferred_element_type=f32)
-        for z in range(LZ):
-            lanes = slice(z * LANES, (z + 1) * LANES)
-            grad = shift_sum([got[b * 8 : (b + 1) * 8, lanes] for b in range(9)])
-            fgs[pl.ds(pl.multiple_of((t * LZ + z) * 8, 8), 8), :] = grad
-        return carry
-
-    lax.fori_loop(0, LT, feature_grad_slice, 0, unroll=True)
+    preact_copies = send_halo(qbuf, send_q, recv_q)
 
     def in_order(parts, count):
         total = parts[0].astype(f32)
@@ -529,6 +520,14 @@
     mid_b[...] = (total * scale).astype(bf16)
     copies_b = to_deep(mid_b, got_b.at[deep], send_b, recv_b)
     got_b[deep] = mid_b[...]
+
+    wt1[...] = lax.dot_general(
+        one_hot(72, 0), first_w[...], nt_dims, preferred_element_type=f32
+    ).astype(bf16)
+
+    x_two = [lk[0:12, :], lk[12:24, :]]
+    y_two = [lk[24:36, :], lk[36:48, :]]
+    pairs = [[sin_cos(psi) for psi in three] for three in loop_phases(x_two, y_two)]
 
     total = gm1[wide_rows(mx, rows1), :]
     for k, copy in enumerate(copies_e):
@@ -538,6 +537,34 @@
     mid_f[...] = total
     copies_f = to_deep(mid_f, got_f.at[deep], send_f, recv_f)
     got_f[deep] = total
+
+    for copy in copies_b:
+        copy.wait()
+    fin_d[...] = in_order(got_b, nd).astype(bf16)
+    copies_d = to_wide(lambda index: fin_d, lambda k: out2.at[wide_rows(mx, rows2)], send_d, recv_d)
+    stores = [pltpu.make_async_copy(fin_d, out2.at[wide_rows(mx, rows2)], out_sem.at[1])]
+    stores[0].start()
+
+    for copy in copies_f:
+        copy.wait()
+    fin_g[...] = in_order(got_f, nd)
+    copies_h = to_wide(lambda index: fin_g, lambda k: out1.at[wide_rows(mx, rows1)], send_h, recv_h)
+    stores.append(pltpu.make_async_copy(fin_g, out1.at[wide_rows(mx, rows1)], out_sem.at[2]))
+    stores[1].start()
+
+    phase_copy.wait()
+    for copy in preact_copies:
+        copy.wait()
+
+    def feature_grad_slice(t, carry):
+        got = jnp.dot(wt1[...], stacked(qbuf, t), preferred_element_type=f32)
+        for z in range(LZ):
+            lanes = slice(z * LANES, (z + 1) * LANES)
+            grad = shift_sum([got[b * 8 : (b + 1) * 8, lanes] for b in range(9)])
+            fgs[pl.ds(pl.multiple_of((t * LZ + z) * 8, 8), 8), :] = grad
+        return carry
+
+    lax.fori_loop(0, LT, feature_grad_slice, 0, unroll=True)
 
     third = 1.0 / 3.0
     loop_grads = []
@@ -571,22 +598,9 @@
         link_out[24 + c * 12 : 36 + c * 12, :] = y_ctx
         link_out[48 + c * 12 : 60 + c * 12, :] = cot[c * 12 : c * 12 + 12, :] - grad + shifted(grad, 0, -1)
 
-    stores = [pltpu.make_async_copy(link_out, out_link, out_sem.at[0])]
-    stores[0].start()
-
-    for copy in copies_b:
-        copy.wait()
-    fin_d[...] = in_order(got_b, nd).astype(bf16)
-    copies_d = to_wide(lambda index: fin_d, lambda k: out2.at[wide_rows(mx, rows2)], send_d, recv_d)
-    stores.append(pltpu.make_async_copy(fin_d, out2.at[wide_rows(mx, rows2)], out_sem.at[1]))
-    stores[1].start()
-
-    for copy in copies_f:
-        copy.wait()
-    fin_g[...] = in_order(got_f, nd)
-    copies_h = to_wide(lambda index: fin_g, lambda k: out1.at[wide_rows(mx, rows1)], send_h, recv_h)
-    stores.append(pltpu.make_async_copy(fin_g, out1.at[wide_rows(mx, rows1)], out_sem.at[2]))
+    stores.append(pltpu.make_async_copy(link_out, out_link, out_sem.at[0]))
     stores[2].start()
+
     for copy in copies_d + stores + copies_h:
         copy.wait()
 

time: 48 us -> 47.5 us (0.990)
  Pallas kernels: 47.2 us -> 46.7 us
    pallas_call x1, Pallas kernels: 45.2 us -> 44.7 us  [local(): pl.pallas_call(functools.partial(main_kernel, scale), out_shape=(jax.Shap...]
where the time goes in v3:
time: 47.5 us; the launch traced here: 47.4 us
  Pallas kernels  46.7 us (98%)
  between operations  0.64 us (1%)
    pallas_call x1, Pallas kernels, local(): pl.pallas_call(functools.partial(main_kernel, scale), out_shape=(jax.Shap...  44.7 us
    pallas_call x1, Pallas kernels, local(): pl.pallas_call(write_kernel, out_shape=(jax.ShapeDtypeStruct((3, 2, LT, L...  1.99 us

profile of v3, /device:TPU:1, one launch (start us, length us, event | category | flops | bytes accessed | tf_op | source)
XLA Modules:
  0.0 47.4 jit_solution(7993118463464216214)
XLA Ops:
  0.6 44.7 %main_kernel.1 = (f32[72,128]{1,0:T(8,128)}, bf16[1024,128]{1,0:T(8,128)(2,1)}, f32[256,128]{1,0:T(8,128)}) custom-call(f32[3,2,3,4,128]{4,3,2,1,0:T(4,128)} %refs_0_.1, s32[3,4,128]{2,1,0:T(4,128)} %refs_1_.1, s32[2,3,4,128]{3,2,1,0:T(4,128)} %refs_2_.1, bf16[288,54]{1,0:T(8,128)(2,1)} %bitcast.9, f32[1,32]{1,0:T(1,128)} %bitcast.10, ...), custom_call_target="tpu_custom_call" | custom-call | tf_op jit(solution)/shard_map/main_kernel/pallas_call | solution.py:644
  45.4 2.0 %write_kernel.1 = (f32[3,2,3,4,128]{4,3,2,1,0:T(4,128)}, f32[288,54]{1,0:T(8,128)}, f32[1,32]{1,0:T(1,128)}, f32[432,288]{1,0:T(8,128)}, f32[1,48]{1,0:T(1,128)}) custom-call(f32[72,128]{1,0:T(8,128)} %get-tuple-element.13.link, bf16[1024,128]{1,0:T(8,128)(2,1)} %get-tuple-element.14.sum2, f32[256,128]{1,0:T(8,128)} %get-tuple-element.15.sum1), custom_call_target="tpu_custom_call" | custom-call | tf_op jit(solution)/shard_map/write_kernel/pallas_call | solution.py:712

commit v4 on v3

--- a/solution.py
+++ b/solution.py
@@ -161,28 +161,27 @@
     for peer in greeted:
         pl.semaphore_signal(barrier, inc=1, device_id=peer, device_id_type=MESH_ID)
 
-    def to_wide(src, dst, send, recv):
-        copies = []
+    def all_of(ref, send, recv, peer):
+        return pltpu.make_async_remote_copy(
+            src_ref=ref, dst_ref=ref, send_sem=send, recv_sem=recv, device_id=peer, device_id_type=MESH_ID
+        )
+
+    def to_wide(src, dst, whole, send, recv):
         for k in wide_order:
             peer = wide_peer(k)
-            copy = pltpu.make_async_remote_copy(
+            pltpu.make_async_remote_copy(
                 src_ref=src(2 * peer[0] + lax.rem(peer[1], 2)), dst_ref=dst(k),
-                send_sem=send.at[k], recv_sem=recv.at[k], device_id=peer, device_id_type=MESH_ID,
-            )
-            copy.start()
-            copies.append(copy)
-        return copies
-
-    def to_deep(src, dst, send, recv):
-        copies = []
+                send_sem=send, recv_sem=recv, device_id=peer, device_id_type=MESH_ID,
+            ).start()
+        return all_of(whole.at[1:nx], send, recv, wide_peer(1))
+
+    def to_deep(src, dst, whole, send, recv):
         for k in deep_order:
-            copy = pltpu.make_async_remote_copy(
+            pltpu.make_async_remote_copy(
                 src_ref=src, dst_ref=dst,
-                send_sem=send.at[k], recv_sem=recv.at[k], device_id=deep_peer(k), device_id_type=MESH_ID,
-            )
-            copy.start()
-            copies.append(copy)
-        return copies
+                send_sem=send, recv_sem=recv, device_id=deep_peer(k), device_id_type=MESH_ID,
+            ).start()
+        return all_of(whole.at[1:nd], send, recv, deep_peer(1))
 
     loads[0].wait()
     for d in range(3):
@@ -401,17 +400,14 @@
     v_into = {-1: slice(5, 6), 0: slice(1, 5), 1: slice(0, 1)}
 
     def send_halo(buf, send, recv):
-        copies = []
-        for i, (dt, dz) in enumerate(DIRS):
-            copy = pltpu.make_async_remote_copy(
+        for dt, dz in DIRS:
+            pltpu.make_async_remote_copy(
                 src_ref=buf.at[h_from[dt], v_from[dz]],
                 dst_ref=buf.at[h_into[dt], v_into[dz]],
-                send_sem=send.at[i], recv_sem=recv.at[i],
+                send_sem=send, recv_sem=recv,
                 device_id=neighbour(dt, dz), device_id_type=MESH_ID,
-            )
-            copy.start()
-            copies.append(copy)
-        return copies
+            ).start()
+        return all_of(buf.at[0:3], send, recv, neighbour(1, 0))
 
     param_copies = send_halo(pbuf, send_p, recv_p)
 
@@ -454,11 +450,10 @@
         return pl.ds(pl.multiple_of(index * rows, rows), rows)
 
     copies_a = to_wide(
-        lambda index: gm2.at[wide_rows(index, rows2)], lambda k: got_a.at[k], send_a, recv_a
-    )
-
-    for copy in param_copies:
-        copy.wait()
+        lambda index: gm2.at[wide_rows(index, rows2)], lambda k: got_a.at[k], got_a, send_a, recv_a
+    )
+
+    param_copies.wait()
 
     def stacked(buf, t):
         rows = []
@@ -502,7 +497,7 @@
     lane = lax.broadcasted_iota(jnp.int32, (112, LANES), 1)
     gm1[144:256, :] = jnp.where(lane == 0, bias, 0.0)
     copies_e = to_wide(
-        lambda index: gm1.at[wide_rows(index, rows1)], lambda k: got_e.at[k], send_e, recv_e
+        lambda index: gm1.at[wide_rows(index, rows1)], lambda k: got_e.at[k], got_e, send_e, recv_e
     )
 
     preact_copies = send_halo(qbuf, send_q, recv_q)
@@ -514,11 +509,11 @@
         return total
 
     total = gm2[wide_rows(mx, rows2), :].astype(f32)
-    for k, copy in enumerate(copies_a):
-        copy.wait()
-        total = total + got_a[wide_order[k]].astype(f32)
+    copies_a.wait()
+    for k in range(1, nx):
+        total = total + got_a[k].astype(f32)
     mid_b[...] = (total * scale).astype(bf16)
-    copies_b = to_deep(mid_b, got_b.at[deep], send_b, recv_b)
+    copies_b = to_deep(mid_b, got_b.at[deep], got_b, send_b, recv_b)
     got_b[deep] = mid_b[...]
 
     wt1[...] = lax.dot_general(
@@ -530,31 +525,28 @@
     pairs = [[sin_cos(psi) for psi in three] for three in loop_phases(x_two, y_two)]
 
     total = gm1[wide_rows(mx, rows1), :]
-    for k, copy in enumerate(copies_e):
-        copy.wait()
-        total = total + got_e[wide_order[k]]
+    copies_e.wait()
+    for k in range(1, nx):
+        total = total + got_e[k]
     total = total * scale
     mid_f[...] = total
-    copies_f = to_deep(mid_f, got_f.at[deep], send_f, recv_f)
+    copies_f = to_deep(mid_f, got_f.at[deep], got_f, send_f, recv_f)
     got_f[deep] = total
 
-    for copy in copies_b:
-        copy.wait()
+    copies_b.wait()
     fin_d[...] = in_order(got_b, nd).astype(bf16)
-    copies_d = to_wide(lambda index: fin_d, lambda k: out2.at[wide_rows(mx, rows2)], send_d, recv_d)
+    copies_d = to_wide(lambda index: fin_d, lambda k: out2.at[wide_rows(mx, rows2)], got_a, send_d, recv_d)
     stores = [pltpu.make_async_copy(fin_d, out2.at[wide_rows(mx, rows2)], out_sem.at[1])]
     stores[0].start()
 
-    for copy in copies_f:
-        copy.wait()
+    copies_f.wait()
     fin_g[...] = in_order(got_f, nd)
-    copies_h = to_wide(lambda index: fin_g, lambda k: out1.at[wide_rows(mx, rows1)], send_h, recv_h)
+    copies_h = to_wide(lambda index: fin_g, lambda k: out1.at[wide_rows(mx, rows1)], got_e, send_h, recv_h)
     stores.append(pltpu.make_async_copy(fin_g, out1.at[wide_rows(mx, rows1)], out_sem.at[2]))
     stores[1].start()
 
     phase_copy.wait()
-    for copy in preact_copies:
-        copy.wait()
+    preact_copies.wait()
 
     def feature_grad_slice(t, carry):
         got = jnp.dot(wt1[...], stacked(qbuf, t), preferred_element_type=f32)
@@ -601,7 +593,7 @@
     stores.append(pltpu.make_async_copy(link_out, out_link, out_sem.at[0]))
     stores[2].start()
 
-    for copy in copies_d + stores + copies_h:
+    for copy in [copies_d] + stores + [copies_h]:
         copy.wait()
 
 
@@ -695,9 +687,8 @@
             mem((nd, rows1, LANES), f32),
             mem((rows1, LANES), f32),
             mem((72, LANES), f32),
-            dma((9,)), dma((3,)), dma((8,)), dma((8,)), dma((8,)), dma((8,)), dma((8,)), dma((8,)), dma, dma,
-            dma((nx,)), dma((nx,)), dma((nd,)), dma((nd,)), dma((nx,)), dma((nx,)),
-            dma((nx,)), dma((nx,)), dma((nd,)), dma((nd,)), dma((nx,)), dma((nx,)),
+            dma((9,)), dma((3,)), dma((8,)), dma((8,)), dma, dma, dma, dma, dma, dma,
+            dma, dma, dma, dma, dma, dma, dma, dma, dma, dma, dma, dma,
         ],
         compiler_params=pltpu.CompilerParams(
             collective_id=0, has_side_effects=True, vmem_limit_bytes=56 * 1024 * 1024

time: 47.5 us -> 44.6 us (0.939)
  Pallas kernels: 46.7 us -> 43.8 us
    pallas_call x1, Pallas kernels: 44.7 us -> 41.8 us  [local(): pl.pallas_call(functools.partial(main_kernel, scale), out_shape=(jax.Shap...]
where the time goes in v4:
time: 44.6 us; the launch traced here: 44.5 us
  Pallas kernels  43.8 us (98%)
  between operations  0.64 us (1%)
    pallas_call x1, Pallas kernels, local(): pl.pallas_call(functools.partial(main_kernel, scale), out_shape=(jax.Shap...  41.8 us
    pallas_call x1, Pallas kernels, local(): pl.pallas_call(write_kernel, out_shape=(jax.ShapeDtypeStruct((3, 2, LT, L...  1.99 us

profile of v4, /device:TPU:1, one launch (start us, length us, event | category | flops | bytes accessed | tf_op | source)
XLA Modules:
  0.0 44.5 jit_solution(5877752417731378170)
XLA Ops:
  0.6 41.8 %main_kernel.1 = (f32[72,128]{1,0:T(8,128)}, bf16[1024,128]{1,0:T(8,128)(2,1)}, f32[256,128]{1,0:T(8,128)}) custom-call(f32[3,2,3,4,128]{4,3,2,1,0:T(4,128)} %refs_0_.1, s32[3,4,128]{2,1,0:T(4,128)} %refs_1_.1, s32[2,3,4,128]{3,2,1,0:T(4,128)} %refs_2_.1, bf16[288,54]{1,0:T(8,128)(2,1)} %bitcast.9, f32[1,32]{1,0:T(1,128)} %bitcast.10, ...), custom_call_target="tpu_custom_call" | custom-call | tf_op jit(solution)/shard_map/main_kernel/pallas_call | solution.py:636
  42.5 2.0 %write_kernel.1 = (f32[3,2,3,4,128]{4,3,2,1,0:T(4,128)}, f32[288,54]{1,0:T(8,128)}, f32[1,32]{1,0:T(1,128)}, f32[432,288]{1,0:T(8,128)}, f32[1,48]{1,0:T(1,128)}) custom-call(f32[72,128]{1,0:T(8,128)} %get-tuple-element.13.link, bf16[1024,128]{1,0:T(8,128)(2,1)} %get-tuple-element.14.sum2, f32[256,128]{1,0:T(8,128)} %get-tuple-element.15.sum1), custom_call_target="tpu_custom_call" | custom-call | tf_op jit(solution)/shard_map/write_kernel/pallas_call | solution.py:703

commit v5 on v4

--- a/solution.py
+++ b/solution.py
@@ -197,16 +197,14 @@
     t_into = {-1: slice(5, 7), 0: slice(2, 5), 1: slice(0, 2)}
     z_from = {-1: slice(8, 16), 0: slice(8, 24), 1: slice(16, 24)}
     z_into = {-1: slice(24, 32), 0: slice(8, 24), 1: slice(0, 8)}
-    link_copies = []
-    for i, (dt, dz) in enumerate(DIRS):
+    for dt, dz in DIRS:
         copy = pltpu.make_async_remote_copy(
             src_ref=lbuf.at[t_from[dt], z_from[dz]],
             dst_ref=lbuf.at[t_into[dt], z_into[dz]],
-            send_sem=send_l.at[i], recv_sem=recv_l.at[i],
+            send_sem=send_l, recv_sem=recv_l,
             device_id=neighbour(dt, dz), device_id_type=MESH_ID,
         )
         copy.start()
-        link_copies.append(copy)
     fs[...] = jnp.zeros_like(fs)
 
     for load in loads[1:]:
@@ -249,8 +247,7 @@
         return jnp.sum(jnp.where(eye, row_ref[...], 0.0), axis=1, keepdims=True)
 
     b1_col, b2_col = as_column(b1, HID), as_column(b2, OUTC)
-    for copy in link_copies:
-        copy.wait()
+    all_of(gm1.at[0:176], send_l, recv_l, neighbour(1, 0)).wait()
 
     def feature_slice(t, carry):
         x_two = [lbuf[t, pl.ds(comp, 8, stride=4), :] for comp in (0, 1)]
@@ -273,8 +270,9 @@
             w1p[...], fcols[pl.ds(pl.multiple_of(t * 80, 16), 240), :], preferred_element_type=f32
         )
         pre = got[0:32, 0:768] + got[32:64, 128:896] + got[64:96, 256:1024] + b1_col
-        pres[t] = pre[:, 128:640]
-        hid = pre / (1.0 + jnp.exp(-pre))
+        sig = 1.0 / (1.0 + jnp.exp(-pre))
+        hid = pre * sig
+        pres[t] = (sig * (1.0 + pre * (1.0 - sig)))[:, 128:640]
         row = pl.multiple_of(t * 288, 16)
         for z in range(6):
             blocks = nine_shifts(hid[:, z * LANES : (z + 1) * LANES])
@@ -467,9 +465,7 @@
         for z in range(LZ):
             lanes = slice(z * LANES, (z + 1) * LANES)
             grad = shift_sum([got[b * HID : (b + 1) * HID, lanes] for b in range(9)])
-            pre = pres[t + 1, :, lanes]
-            sig = 1.0 / (1.0 + jnp.exp(-pre))
-            grad = grad * (sig * (1.0 + pre * (1.0 - sig)))
+            grad = grad * pres[t + 1, :, lanes]
             qbuf[t + 1, z + 1] = grad.astype(bf16)
             total = total + grad
         return total
@@ -496,12 +492,6 @@
     bias = jnp.concatenate([bias2, bias1, jnp.zeros((32, 1), f32)], axis=0)
     lane = lax.broadcasted_iota(jnp.int32, (112, LANES), 1)
     gm1[144:256, :] = jnp.where(lane == 0, bias, 0.0)
-    copies_e = to_wide(
-        lambda index: gm1.at[wide_rows(index, rows1)], lambda k: got_e.at[k], got_e, send_e, recv_e
-    )
-
-    preact_copies = send_halo(qbuf, send_q, recv_q)
-
     def in_order(parts, count):
         total = parts[0].astype(f32)
         for k in range(1, count):
@@ -515,6 +505,12 @@
     mid_b[...] = (total * scale).astype(bf16)
     copies_b = to_deep(mid_b, got_b.at[deep], got_b, send_b, recv_b)
     got_b[deep] = mid_b[...]
+
+    copies_e = to_wide(
+        lambda index: gm1.at[wide_rows(index, rows1)], lambda k: got_e.at[k], got_e, send_e, recv_e
+    )
+
+    preact_copies = send_halo(qbuf, send_q, recv_q)
 
     wt1[...] = lax.dot_general(
         one_hot(72, 0), first_w[...], nt_dims, preferred_element_type=f32
@@ -687,7 +683,7 @@
             mem((nd, rows1, LANES), f32),
             mem((rows1, LANES), f32),
             mem((72, LANES), f32),
-            dma((9,)), dma((3,)), dma((8,)), dma((8,)), dma, dma, dma, dma, dma, dma,
+            dma((9,)), dma((3,)), dma, dma, dma, dma, dma, dma, dma, dma,
             dma, dma, dma, dma, dma, dma, dma, dma, dma, dma, dma, dma,
         ],
         compiler_params=pltpu.CompilerParams(

time: 44.6 us -> 44.6 us (level)
  no operation moved by 1% of the time
where the time goes in v5:
time: 44.6 us; the launch traced here: 44.4 us
  Pallas kernels  43.8 us (98%)
  between operations  0.64 us (1%)
    pallas_call x1, Pallas kernels, local(): pl.pallas_call(functools.partial(main_kernel, scale), out_shape=(jax.Shap...  41.8 us
    pallas_call x1, Pallas kernels, local(): pl.pallas_call(write_kernel, out_shape=(jax.ShapeDtypeStruct((3, 2, LT, L...  1.99 us

profile of v5, /device:TPU:1, one launch (start us, length us, event | category | flops | bytes accessed | tf_op | source)
XLA Modules:
  0.0 44.4 jit_solution(554955256930509728)
XLA Ops:
  0.6 41.8 %main_kernel.1 = (f32[72,128]{1,0:T(8,128)}, bf16[1024,128]{1,0:T(8,128)(2,1)}, f32[256,128]{1,0:T(8,128)}) custom-call(f32[3,2,3,4,128]{4,3,2,1,0:T(4,128)} %refs_0_.1, s32[3,4,128]{2,1,0:T(4,128)} %refs_1_.1, s32[2,3,4,128]{3,2,1,0:T(4,128)} %refs_2_.1, bf16[288,54]{1,0:T(8,128)(2,1)} %bitcast.9, f32[1,32]{1,0:T(1,128)} %bitcast.10, ...), custom_call_target="tpu_custom_call" | custom-call | tf_op jit(solution)/shard_map/main_kernel/pallas_call | solution.py:632
  42.4 2.0 %write_kernel.1 = (f32[3,2,3,4,128]{4,3,2,1,0:T(4,128)}, f32[288,54]{1,0:T(8,128)}, f32[1,32]{1,0:T(1,128)}, f32[432,288]{1,0:T(8,128)}, f32[1,48]{1,0:T(1,128)}) custom-call(f32[72,128]{1,0:T(8,128)} %get-tuple-element.13.link, bf16[1024,128]{1,0:T(8,128)(2,1)} %get-tuple-element.14.sum2, f32[256,128]{1,0:T(8,128)} %get-tuple-element.15.sum1), custom_call_target="tpu_custom_call" | custom-call | tf_op jit(solution)/shard_map/write_kernel/pallas_call | solution.py:699
